TPU v7x, 512 devices: a whole 4x8x8 slice. The times are simulated.
512 devices in a mesh: depth: 32 (over y, x), plane: 16 (over z, core).
Axes of the slice: x: 4, y: 8, z: 8, core: 2. Of those that a mesh axis runs over, the one named last changes fastest.
Arguments:
- activations: bfloat16 [32, 32, 64, 1024], P('plane', 'depth'), may hold values from -6 to 6
- plane_weight: bfloat16 [2, 3, 64, 576], replicated, may hold values from -0.375 to 0.375
- plane_bias: float32 [2, 3, 64], replicated, may hold values from -3 to 3
- depth_weight: bfloat16 [2, 64, 192], replicated, may hold values from -0.75 to 0.75
- depth_bias: float32 [2, 64], replicated, may hold values from -3 to 3
- counts: int32 [16], replicated, may hold values from 1 to 2, as said below
- neighbours: int32 [32, 8], P('plane'), may hold values from -1 to 31, as said below
- voxel_mask: int32 [32, 32, 1024], P('plane', 'depth'), may hold values from 0 to 1, as said below
Outputs:
- hidden: bfloat16 [32, 32, 64, 1024], P('plane', 'depth')
Inputs may be any that keep to these rules, and one draw needn't show every extreme that they name: `counts`: each entry is between 1 and 2; at least one entry equals 2. `neighbours`: for a live slot, the live slot that holds the adjacent tile of a grid in that direction, or -1; all -1 for dead slots; neighbourhood is symmetric. `voxel_mask`: zero in dead slots.
All inputs are finite; a program needn't handle non-finite values.
Results may differ from a plain program's by a relative error of at most 0.008.
Values may be sent and summed in bfloat16 or wider, within the bound.
A program may use at most 64 MiB of HBM per device.

v0:
```python
import jax
import jax.numpy as jnp
from jax import lax
from jax.sharding import PartitionSpec as P

TILE = 32
BLOCKS = 2


def laid_out(pieces, dim):
    shape = list(pieces.shape[1:])
    shape[dim] *= pieces.shape[0]
    return jnp.moveaxis(pieces, 0, dim).reshape(shape)


def copy_for_each(shard, axis):
    count = lax.axis_size(axis)
    return lax.all_to_all(
        jnp.broadcast_to(shard[None], (count, *shard.shape)), axis, 0, 0, tiled=True
    )


def gather_directly(shard, axis, dim):
    return laid_out(copy_for_each(shard, axis), dim)


def with_halo(cells, sides, width):
    for axis, dim in sides:
        count = lax.axis_size(axis)
        ends = count - 1
        head = lax.slice_in_dim(cells, 0, width, axis=dim)
        tail = lax.slice_in_dim(cells, cells.shape[dim] - width, cells.shape[dim], axis=dim)
        cells = jnp.concatenate(
            [
                lax.ppermute(tail, axis, [(i, (i + 1) % count) for i in range(ends)]),
                cells,
                lax.ppermute(head, axis, [((i + 1) % count, i) for i in range(ends)]),
            ],
            axis=dim,
        )
    return cells


def flatten(array):
    return array.reshape(array.shape[:-2] + (-1,))


def strips(tile_view, strip_width):
    top_rows = tile_view[..., :strip_width, :]
    bottom = tile_view[..., TILE - strip_width :, :]
    left_cols = tile_view[..., :, :strip_width]
    right_cols = tile_view[..., :, TILE - strip_width :]
    return jnp.concatenate(
        [flatten(top_rows), flatten(bottom), flatten(left_cols), flatten(right_cols)], -1
    )


def surround(center, neighbour_table, strip_pool, strip_width):
    length = strip_width * TILE
    present = neighbour_table >= 0
    safe_index = jnp.maximum(neighbour_table, 0)

    def fetch_strip(column, segment, piece_shape):
        pieces = strip_pool[safe_index[:, column]][..., segment * length : (segment + 1) * length]
        pieces = pieces.reshape(pieces.shape[:-1] + piece_shape)
        keep = present[:, column].reshape((-1,) + (1,) * (pieces.ndim - 1))
        return jnp.where(keep, pieces, jnp.zeros_like(pieces))

    rows_shape = (strip_width, TILE)
    cols_shape = (TILE, strip_width)
    north_west = fetch_strip(0, 1, rows_shape)[..., TILE - strip_width :]
    north = fetch_strip(1, 1, rows_shape)
    north_east = fetch_strip(2, 1, rows_shape)[..., :strip_width]
    west_side = fetch_strip(3, 3, cols_shape)
    east_side = fetch_strip(4, 2, cols_shape)
    south_west = fetch_strip(5, 0, rows_shape)[..., TILE - strip_width :]
    south_side = fetch_strip(6, 0, rows_shape)
    south_east = fetch_strip(7, 0, rows_shape)[..., :strip_width]
    upper_band = jnp.concatenate([north_west, north, north_east], -1)
    middle = jnp.concatenate([west_side, center, east_side], -1)
    lower_band = jnp.concatenate([south_west, south_side, south_east], -1)
    return jnp.concatenate([upper_band, middle, lower_band], -2)


def plane_conv(padded, weight):
    side = padded.shape[-1]
    inner = side - 2
    span = inner * side
    length = -(-span // 128) * 128
    flat = padded.reshape(padded.shape[:-2] + (side * side,))
    extra = length + 2 * side + 2 - side * side
    flat = jnp.pad(flat, [(0, 0)] * (flat.ndim - 1) + [(0, extra)])
    channels = weight.shape[0]
    total = None
    for row_off in range(3):
        for col_off in range(3):
            tap = row_off * 3 + col_off
            start = row_off * side + col_off
            view = flat[..., start : start + length]
            term = jnp.einsum(
                "ok,nskq->nsoq",
                weight[:, tap * channels : (tap + 1) * channels],
                view,
                preferred_element_type=jnp.float32,
            )
            total = term if total is None else total + term
    result = total[..., :span].reshape(total.shape[:-1] + (inner, side))[..., :inner]
    return result.reshape(result.shape[:-2] + (inner * inner,))


def activate(summed, offsets, layer_mask):
    return (layer_mask * jax.nn.silu(summed + offsets[:, None])).astype(jnp.bfloat16)


def shards(
    activations, plane_weight, plane_bias, depth_weight, depth_bias, counts, neighbours, voxel_mask
):
    slots = activations.shape[0]
    owner_id = lax.axis_index("plane")
    own_count = jnp.sum(
        jnp.where(jnp.arange(counts.shape[0], dtype=jnp.int32) == owner_id, counts, 0)
    )
    alive = jnp.arange(slots, dtype=jnp.int32) < own_count
    hidden = jnp.where(alive[:, None, None, None], activations, jnp.zeros_like(activations))
    mask_f = voxel_mask.astype(jnp.float32)[:, :, None, :]
    mask_tiles = voxel_mask.reshape(voxel_mask.shape[:-1] + (TILE, TILE))
    mask_pool = gather_directly(strips(mask_tiles, 2), "plane", 0)
    mask_wide = surround(mask_tiles, neighbours, mask_pool, 2).astype(jnp.float32)[:, :, None]
    for block_id in range(BLOCKS):
        tiles_view = hidden.reshape(hidden.shape[:-1] + (TILE, TILE))
        wide_pool = gather_directly(strips(tiles_view, 3), "plane", 0)
        padded = surround(tiles_view, neighbours, wide_pool, 3)
        for layer_id in range(3):
            summed = plane_conv(padded, plane_weight[block_id, layer_id])
            inner = padded.shape[-1] - 2
            margin = (mask_wide.shape[-1] - inner) // 2
            layer_mask = mask_wide[..., margin : margin + inner, margin : margin + inner]
            layer_mask = layer_mask.reshape(layer_mask.shape[:-2] + (inner * inner,))
            padded = activate(summed, plane_bias[block_id, layer_id], layer_mask).reshape(
                summed.shape[:-1] + (inner, inner)
            )
        branch = padded.reshape(hidden.shape)
        extended = with_halo(branch, (("depth", 1),), 1)
        stacked = jnp.concatenate([extended[:, :-2], extended[:, 1:-1], extended[:, 2:]], axis=2)
        summed = jnp.einsum(
            "ok,nskq->nsoq", depth_weight[block_id], stacked, preferred_element_type=jnp.float32
        )
        hidden = (
            hidden.astype(jnp.float32) + mask_f * (summed + depth_bias[block_id][:, None])
        ).astype(jnp.bfloat16)
    return hidden


def solution(mesh):
    in_specs = (
        P("plane", "depth", None, None),
        P(),
        P(),
        P(),
        P(),
        P(),
        P("plane", None),
        P("plane", "depth", None),
    )
    out_specs = P("plane", "depth", None, None)
    return jax.shard_map(shards, mesh=mesh, in_specs=in_specs, out_specs=out_specs, check_vma=False)
```

profile of v0, /device:TPU:31, one launch (start us, length us, event | category | flops | bytes accessed | tf_op | source)
XLA Modules:
  0.0 197.4 jit_solution(7214270699093100674)
XLA Ops:
  0.0 1.4 fusion.196
  2.6 11.0 %all-to-all-start = ((s32[16,2,1,256]{3,1,2,0:T(2,128)}), s32[16,2,1,256]{3,1,2,0:T(2,128)S(1)}, u32[]{:S(2)}, u32[]{:S(2)}) async-start(s32[16,2,1,256]{3,1,2,0:T(2,128)} %broadcast_in_dim.204), calls=%async_computation | async-start | bytes 65536 | tf_op jit(solution)/shard_map/all_to_all | solution.py:18
  13.6 1.3 fusion.151
  15.6 1.0 bitcast_select_fusion
  17.8 3.2 %all-to-all-done = s32[16,2,1,256]{3,1,2,0:T(2,128)S(1)} async-done(((s32[16,2,1,256]{3,1,2,0:T(2,128)}), s32[16,2,1,256]{3,1,2,0:T(2,128)S(1)}, u32[]{:S(2)}, u32[]{:S(2)}) %all-to-all-start) | async-done | bytes 32800 | tf_op jit(solution)/shard_map/all_to_all | solution.py:18
  21.0 1.4 broadcast_in_dim.221
  22.4 4.1 %all-to-all-start.1 = ((bf16[16,2,1,64,384]{4,3,1,2,0:T(8,128)(2,1)}), bf16[16,2,1,64,384]{4,3,1,2,0:T(8,128)(2,1)S(1)}, u32[]{:S(2)}, u32[]{:S(2)}) async-start(bf16[16,2,1,64,384]{4,3,1,2,0:T(8,128)(2,1)} %broadcast_in_dim.221), calls=%async_computation.1 | async-start | bytes 3145728 | tf_op jit(solution)/shard_map/all_to_all | solution.py:18
  34.4 0.7 convert_element_type.115
  35.1 0.7 mul.189
  35.9 29.1 %all-to-all-done.1 = bf16[16,2,1,64,384]{4,3,1,2,0:T(8,128)(2,1)S(1)} async-done(((bf16[16,2,1,64,384]{4,3,1,2,0:T(8,128)(2,1)}), bf16[16,2,1,64,384]{4,3,1,2,0:T(8,128)(2,1)S(1)}, u32[]{:S(2)}, u32[]{:S(2)}) %all-to-all-start.1) | async-done | bytes 1572896 | tf_op jit(solution)/shard_map/all_to_all | solution.py:18
  65.6 1.2 gather_fusion.11
  67.4 1.2 gather_fusion.9
  68.6 0.7 gather_fusion.13
  69.3 0.7 gather_fusion.10
  70.0 0.7 gather_fusion.8
  70.7 0.7 gather_fusion.15
  71.7 0.8 slice.938
  73.0 0.9 slice.935
  74.2 0.8 slice_select_fusion.5
  75.2 0.7 slice_select_fusion.6
  80.8 1.0 copy.133
  81.9 1.4 copy.134
  86.4 1.1 copy.135
  87.6 1.2 copy.136
  91.8 1.1 copy.137
  93.9 4.3 %collective-permute-start = (bf16[2,1,64,1024]{3,2,0,1:T(8,128)(2,1)S(1)}, bf16[2,1,64,1024]{3,2,0,1:T(8,128)(2,1)S(1)}, u32[]{:S(2)}, u32[]{:S(2)}) collective-permute-start(bf16[2,1,64,1024]{3,2,0,1:T(8,128)(2,1)S(1)} %multiply_convert_fusion.5), channel_id=1, source_target_pairs={{0,16},{16,32},{32,48},{48,64},{64,80},{80,96},{96,112},{112,128},... | collective-permute-start | bytes 786440 | tf_op jit(solution)/shard_map/ppermute | solution.py:35
  98.2 1.9 collective-permute-start.1
  100.2 4.1 %collective-permute-done = bf16[2,1,64,1024]{3,2,0,1:T(8,128)(2,1)S(1)} collective-permute-done((bf16[2,1,64,1024]{3,2,0,1:T(8,128)(2,1)S(1)}, bf16[2,1,64,1024]{3,2,0,1:T(8,128)(2,1)S(1)}, u32[]{:S(2)}, u32[]{:S(2)}) %collective-permute-start) | collective-permute-done | bytes 262176 | tf_op jit(solution)/shard_map/ppermute | solution.py:35
  104.3 7.2 %collective-permute-done.1 = bf16[2,1,64,1024]{3,2,0,1:T(8,128)(2,1)S(1)} collective-permute-done((bf16[2,1,64,1024]{3,2,0,1:T(8,128)(2,1)S(1)}, bf16[2,1,64,1024]{3,2,0,1:T(8,128)(2,1)S(1)}, u32[]{:S(2)}, u32[]{:S(2)}) %collective-permute-start.1) | collective-permute-done | bytes 262176 | tf_op jit(solution)/shard_map/ppermute | solution.py:37
  112.9 44.1 %all_to_all.15 = bf16[16,2,1,64,384]{4,3,1,2,0:T(8,128)(2,1)S(1)} all-to-all(bf16[16,2,1,64,384]{4,3,1,2,0:T(8,128)(2,1)S(1)} %broadcast_in_dim.230), channel_id=1, replica_groups=mesh['depth'=32,'plane'=16] {'plane'}, dimensions={0} | all-to-all | bytes 3145728 | tf_op jit(solution)/shard_map/all_to_all | solution.py:18
  157.0 0.7 gather_fusion.20
  157.7 0.7 gather_fusion.19
  158.4 0.7 gather_fusion.22
  159.1 0.7 gather_fusion.17
  159.8 0.7 gather_fusion.21
  160.5 0.7 gather_fusion.18
  161.2 0.7 gather_fusion.16
  161.9 0.7 gather_fusion.23
  169.1 1.0 copy.161
  170.2 1.4 copy.162
  174.7 1.1 copy.163
  175.9 1.0 copy.164
  180.0 1.1 copy.165
  182.0 1.9 collective-permute-start.2
  183.9 3.4 %collective-permute-start.3 = (bf16[2,1,64,1024]{3,2,0,1:T(8,128)(2,1)S(1)}, bf16[2,1,64,1024]{3,2,0,1:T(8,128)(2,1)S(1)}, u32[]{:S(2)}, u32[]{:S(2)}) collective-permute-start(bf16[2,1,64,1024]{3,2,0,1:T(8,128)(2,1)S(1)} %multiply_convert_fusion.4), channel_id=1, source_target_pairs={{16,0},{32,16},{48,32},{64,48},{80,64},{96,80},{112,96},{128,112},... | collective-permute-start | bytes 786440 | tf_op jit(solution)/shard_map/ppermute | solution.py:37
  187.3 4.2 %collective-permute-done.2 = bf16[2,1,64,1024]{3,2,0,1:T(8,128)(2,1)S(1)} collective-permute-done((bf16[2,1,64,1024]{3,2,0,1:T(8,128)(2,1)S(1)}, bf16[2,1,64,1024]{3,2,0,1:T(8,128)(2,1)S(1)}, u32[]{:S(2)}, u32[]{:S(2)}) %collective-permute-start.2) | collective-permute-done | bytes 262176 | tf_op jit(solution)/shard_map/ppermute | solution.py:35
  191.5 5.0 %collective-permute-done.3 = bf16[2,1,64,1024]{3,2,0,1:T(8,128)(2,1)S(1)} collective-permute-done((bf16[2,1,64,1024]{3,2,0,1:T(8,128)(2,1)S(1)}, bf16[2,1,64,1024]{3,2,0,1:T(8,128)(2,1)S(1)}, u32[]{:S(2)}, u32[]{:S(2)}) %collective-permute-start.3) | collective-permute-done | bytes 262176 | tf_op jit(solution)/shard_map/ppermute | solution.py:37
  196.4 1.0 fusion.16
  (289 shorter events, 39.2 us)
Async XLA Ops:
  0.0 17.0 %copy-start.38 = (s32[2,8]{1,0:T(2,128)S(1)}, s32[2,8]{1,0:T(2,128)}, u32[]{:S(2)}) copy-start(s32[2,8]{1,0:T(2,128)} %param.14) | copy-start | bytes 196
  2.6 18.4 %all-to-all-start = ((s32[16,2,1,256]{3,1,2,0:T(2,128)}), s32[16,2,1,256]{3,1,2,0:T(2,128)S(1)}, u32[]{:S(2)}, u32[]{:S(2)}) async-start(s32[16,2,1,256]{3,1,2,0:T(2,128)} %broadcast_in_dim.204), calls=%async_computation | async-start | bytes 65536 | tf_op jit(solution)/shard_map/all_to_all | solution.py:18
  17.7 14.9 %copy-start.23 = (s32[1024]{0:T(1024)}, s32[1024]{0:T(1024)S(1)}, u32[]{:S(2)}) copy-start(s32[1024]{0:T(1024)S(1)} %get-tuple-element.51) | copy-start | bytes 12292
  17.7 47.3 %copy-start.26 = (s32[1024]{0:T(1024)}, s32[1024]{0:T(1024)S(1)}, u32[]{:S(2)}) copy-start(s32[1024]{0:T(1024)S(1)} %get-tuple-element.52) | copy-start | bytes 12292
  17.8 12.7 %copy-start.24 = (s32[1024]{0:T(1024)}, s32[1024]{0:T(1024)S(1)}, u32[]{:S(2)}) copy-start(s32[1024]{0:T(1024)S(1)} %get-tuple-element.54) | copy-start | bytes 12292
  17.8 47.8 %copy-start.27 = (s32[1024]{0:T(1024)}, s32[1024]{0:T(1024)S(1)}, u32[]{:S(2)}) copy-start(s32[1024]{0:T(1024)S(1)} %get-tuple-element.53) | copy-start | bytes 12292
  17.8 14.1 %copy-start.25 = (s32[1024]{0:T(1024)}, s32[1024]{0:T(1024)S(1)}, u32[]{:S(2)}) copy-start(s32[1024]{0:T(1024)S(1)} %get-tuple-element.49) | copy-start | bytes 12292
  17.8 49.0 %copy-start.28 = (s32[1024]{0:T(1024)}, s32[1024]{0:T(1024)S(1)}, u32[]{:S(2)}) copy-start(s32[1024]{0:T(1024)S(1)} %get-tuple-element.50) | copy-start | bytes 12292
  22.4 4.5 %copy-start.31 = (f32[2,3,64]{2,0,1:T(2,128)S(1)}, f32[2,3,64]{2,0,1:T(2,128)}, u32[]{:S(2)}) copy-start(f32[2,3,64]{2,0,1:T(2,128)} %param.10) | copy-start | bytes 4612
  22.4 5.2 %copy-start = (bf16[2,3,64,576]{3,2,1,0:T(8,128)(2,1)S(1)}, bf16[2,3,64,576]{3,2,1,0:T(8,128)(2,1)}, u32[]{:S(2)}) copy-start(bf16[2,3,64,576]{3,2,1,0:T(8,128)(2,1)} %param.9) | copy-start | bytes 1327108
  22.4 42.6 %all-to-all-start.1 = ((bf16[16,2,1,64,384]{4,3,1,2,0:T(8,128)(2,1)}), bf16[16,2,1,64,384]{4,3,1,2,0:T(8,128)(2,1)S(1)}, u32[]{:S(2)}, u32[]{:S(2)}) async-start(bf16[16,2,1,64,384]{4,3,1,2,0:T(8,128)(2,1)} %broadcast_in_dim.221), calls=%async_computation.1 | async-start | bytes 3145728 | tf_op jit(solution)/shard_map/all_to_all | solution.py:18
  26.6 40.8 %copy-start.29 = (s32[1024]{0:T(1024)}, s32[1024]{0:T(1024)S(1)}, u32[]{:S(2)}) copy-start(s32[1024]{0:T(1024)S(1)} %get-tuple-element.56) | copy-start | bytes 12292
  26.6 40.8 %copy-start.30 = (s32[1024]{0:T(1024)}, s32[1024]{0:T(1024)S(1)}, u32[]{:S(2)}) copy-start(s32[1024]{0:T(1024)S(1)} %get-tuple-element.55) | copy-start | bytes 12292
  26.9 40.5 %copy-start.19 = (pred[2]{0:T(512)(128)(4,1)}, pred[2]{0:T(512)(128)(4,1)S(1)}, u32[]{:S(2)}) copy-start(pred[2]{0:T(512)(128)(4,1)S(1)} %get-tuple-element.19) | copy-start | bytes 10
  26.9 40.5 %copy-start.21 = (pred[2]{0:T(512)(128)(4,1)}, pred[2]{0:T(512)(128)(4,1)S(1)}, u32[]{:S(2)}) copy-start(pred[2]{0:T(512)(128)(4,1)S(1)} %get-tuple-element.16) | copy-start | bytes 10
  26.9 44.7 %copy-start.9 = (pred[2]{0:T(512)(128)(4,1)}, pred[2]{0:T(512)(128)(4,1)S(1)}, u32[]{:S(2)}) copy-start(pred[2]{0:T(512)(128)(4,1)S(1)} %get-tuple-element.17) | copy-start | bytes 10
  26.9 45.7 %copy-start.7 = (pred[2]{0:T(512)(128)(4,1)}, pred[2]{0:T(512)(128)(4,1)S(1)}, u32[]{:S(2)}) copy-start(pred[2]{0:T(512)(128)(4,1)S(1)} %get-tuple-element.18) | copy-start | bytes 10
  27.0 46.0 %copy-start.13 = (pred[2]{0:T(512)(128)(4,1)}, pred[2]{0:T(512)(128)(4,1)S(1)}, u32[]{:S(2)}) copy-start(pred[2]{0:T(512)(128)(4,1)S(1)} %get-tuple-element.15) | copy-start | bytes 10
  27.0 47.1 %copy-start.11 = (pred[2]{0:T(512)(128)(4,1)}, pred[2]{0:T(512)(128)(4,1)S(1)}, u32[]{:S(2)}) copy-start(pred[2]{0:T(512)(128)(4,1)S(1)} %get-tuple-element.20) | copy-start | bytes 10
  27.0 49.1 %copy-start.17 = (pred[2]{0:T(512)(128)(4,1)}, pred[2]{0:T(512)(128)(4,1)S(1)}, u32[]{:S(2)}) copy-start(pred[2]{0:T(512)(128)(4,1)S(1)} %get-tuple-element.13) | copy-start | bytes 10
  27.0 49.3 %copy-start.15 = (pred[2]{0:T(512)(128)(4,1)}, pred[2]{0:T(512)(128)(4,1)S(1)}, u32[]{:S(2)}) copy-start(pred[2]{0:T(512)(128)(4,1)S(1)} %get-tuple-element.14) | copy-start | bytes 10
  81.9 1.4 copy-start.3
  81.9 1.4 copy-start.35
  87.5 1.3 copy-start.5
  87.5 1.3 copy-start.33
  93.0 0.7 copy-start.37
  93.1 7.0 %copy-start.6 = (f32[2,1,1024]{2,1,0:T(1,128)S(1)}, f32[2,1,1024]{2,1,0:T(1,128)}, u32[]{:S(2)}) copy-start(f32[2,1,1024]{2,1,0:T(1,128)} %get-tuple-element.39) | copy-start | bytes 24580
  93.1 7.0 %copy-start.39 = (f32[2,64]{1,0:T(2,128)S(1)}, f32[2,64]{1,0:T(2,128)}, u32[]{:S(2)}) copy-start(f32[2,64]{1,0:T(2,128)} %param.12) | copy-start | bytes 1540
  93.1 18.4 %copy-start.40 = (bf16[2,64,192]{2,1,0:T(8,128)(2,1)S(1)}, bf16[2,64,192]{2,1,0:T(8,128)(2,1)}, u32[]{:S(2)}) copy-start(bf16[2,64,192]{2,1,0:T(8,128)(2,1)} %param.11) | copy-start | bytes 147460
  93.9 10.4 %collective-permute-start = (bf16[2,1,64,1024]{3,2,0,1:T(8,128)(2,1)S(1)}, bf16[2,1,64,1024]{3,2,0,1:T(8,128)(2,1)S(1)}, u32[]{:S(2)}, u32[]{:S(2)}) collective-permute-start(bf16[2,1,64,1024]{3,2,0,1:T(8,128)(2,1)S(1)} %multiply_convert_fusion.5), channel_id=1, source_target_pairs={{0,16},{16,32},{32,48},{48,64},{64,80},{80,96},{96,112},{112,128},... | collective-permute-start | bytes 786440 | tf_op jit(solution)/shard_map/ppermute | solution.py:35
  98.2 13.3 %collective-permute-start.1 = (bf16[2,1,64,1024]{3,2,0,1:T(8,128)(2,1)S(1)}, bf16[2,1,64,1024]{3,2,0,1:T(8,128)(2,1)S(1)}, u32[]{:S(2)}, u32[]{:S(2)}) collective-permute-start(bf16[2,1,64,1024]{3,2,0,1:T(8,128)(2,1)S(1)} %multiply_convert_fusion.5), channel_id=1, source_target_pairs={{16,0},{32,16},{48,32},{64,48},{80,64},{96,80},{112,96},{128,112},... | collective-permute-start | bytes 786440 | tf_op jit(solution)/shard_map/ppermute | solution.py:37
  111.7 0.7 copy-start.1
  157.0 5.8 %copy-start.10 = (pred[2]{0:T(512)(128)(4,1)S(1)}, pred[2]{0:T(512)(128)(4,1)}, u32[]{:S(2)}) copy-start(pred[2]{0:T(512)(128)(4,1)} %copy-done.9) | copy-start | bytes 10
  157.0 6.1 %copy-start.8 = (pred[2]{0:T(512)(128)(4,1)S(1)}, pred[2]{0:T(512)(128)(4,1)}, u32[]{:S(2)}) copy-start(pred[2]{0:T(512)(128)(4,1)} %copy-done.7) | copy-start | bytes 10
  157.0 6.4 %copy-start.14 = (pred[2]{0:T(512)(128)(4,1)S(1)}, pred[2]{0:T(512)(128)(4,1)}, u32[]{:S(2)}) copy-start(pred[2]{0:T(512)(128)(4,1)} %copy-done.13) | copy-start | bytes 10
  157.0 6.7 %copy-start.12 = (pred[2]{0:T(512)(128)(4,1)S(1)}, pred[2]{0:T(512)(128)(4,1)}, u32[]{:S(2)}) copy-start(pred[2]{0:T(512)(128)(4,1)} %copy-done.11) | copy-start | bytes 10
  157.0 6.9 %copy-start.22 = (pred[2]{0:T(512)(128)(4,1)S(1)}, pred[2]{0:T(512)(128)(4,1)}, u32[]{:S(2)}) copy-start(pred[2]{0:T(512)(128)(4,1)} %copy-done.21) | copy-start | bytes 10
  157.0 7.1 %copy-start.20 = (pred[2]{0:T(512)(128)(4,1)S(1)}, pred[2]{0:T(512)(128)(4,1)}, u32[]{:S(2)}) copy-start(pred[2]{0:T(512)(128)(4,1)} %copy-done.19) | copy-start | bytes 10
  157.0 7.4 %copy-start.18 = (pred[2]{0:T(512)(128)(4,1)S(1)}, pred[2]{0:T(512)(128)(4,1)}, u32[]{:S(2)}) copy-start(pred[2]{0:T(512)(128)(4,1)} %copy-done.17) | copy-start | bytes 10
  157.7 6.9 %copy-start.16 = (pred[2]{0:T(512)(128)(4,1)S(1)}, pred[2]{0:T(512)(128)(4,1)}, u32[]{:S(2)}) copy-start(pred[2]{0:T(512)(128)(4,1)} %copy-done.15) | copy-start | bytes 10
  170.2 1.4 copy-start.4
  170.2 1.4 copy-start.34
  175.8 1.1 copy-start.32
  181.1 0.7 copy-start.36
  181.2 15.2 %copy-start.2 = (bf16[2,1,64,1024]{3,2,0,1:T(8,128)(2,1)S(1)}, bf16[2,1,64,1024]{3,2,0,1:T(8,128)(2,1)}, u32[]{:S(2)}) copy-start(bf16[2,1,64,1024]{3,2,0,1:T(8,128)(2,1)} %copy-done.1) | copy-start | bytes 786436
  181.2 15.2 %copy-start.41 = (bf16[2,64,192]{2,1,0:T(8,128)(2,1)S(1)}, bf16[2,64,192]{2,1,0:T(8,128)(2,1)}, u32[]{:S(2)}) copy-start(bf16[2,64,192]{2,1,0:T(8,128)(2,1)} %param.11) | copy-start | bytes 147460
  182.0 9.5 %collective-permute-start.2 = (bf16[2,1,64,1024]{3,2,0,1:T(8,128)(2,1)S(1)}, bf16[2,1,64,1024]{3,2,0,1:T(8,128)(2,1)S(1)}, u32[]{:S(2)}, u32[]{:S(2)}) collective-permute-start(bf16[2,1,64,1024]{3,2,0,1:T(8,128)(2,1)S(1)} %multiply_convert_fusion.4), channel_id=1, source_target_pairs={{0,16},{16,32},{32,48},{48,64},{64,80},{80,96},{96,112},{112,128},... | collective-permute-start | bytes 786440 | tf_op jit(solution)/shard_map/ppermute | solution.py:35
  183.9 12.5 %collective-permute-start.3 = (bf16[2,1,64,1024]{3,2,0,1:T(8,128)(2,1)S(1)}, bf16[2,1,64,1024]{3,2,0,1:T(8,128)(2,1)S(1)}, u32[]{:S(2)}, u32[]{:S(2)}) collective-permute-start(bf16[2,1,64,1024]{3,2,0,1:T(8,128)(2,1)S(1)} %multiply_convert_fusion.4), channel_id=1, source_target_pairs={{16,0},{32,16},{48,32},{64,48},{80,64},{96,80},{112,96},{128,112},... | collective-permute-start | bytes 786440 | tf_op jit(solution)/shard_map/ppermute | solution.py:37
where the time goes:
time: 198 us; the launch traced here: 197 us
  waiting for transfers between devices  52.8 us (27%)
  blocking collectives  44.1 us (22%)
  local copies, waits for them, and re-layouts  43.6 us (22%)
  starting transfers between devices  26.7 us (13%)
  matrix products  17.8 us (9%)
  other arithmetic  10.7 us (5%)
    all_to_all x1, blocking collectives, copy_for_each(): lax.all_to_all(jnp.broadcast_to(shard[None], (count, *shard.shape)), axis...  44.1 us
    all_to_all x2, waiting for transfers between devices, copy_for_each(): lax.all_to_all(jnp.broadcast_to(shard[None], (count, *shard.shape)), axis...  32.4 us
    dot_general x54, matrix products, plane_conv(): jnp.einsum('ok,nskq->nsoq', weight[:, tap * channels:(tap + 1) * channels...  16.6 us
    gather x24, local copies, waits for them, and re-layouts, fetch_strip(): strip_pool[safe_index[:, column]]  16.3 us
    all_to_all x2, starting transfers between devices, copy_for_each(): lax.all_to_all(jnp.broadcast_to(shard[None], (count, *shard.shape)), axis...  15.1 us
    ppermute x2, waiting for transfers between devices, with_halo(): lax.ppermute(head, axis, [((i + 1) % count, i) for i in range(ends)])  12.1 us
    ppermute x2, waiting for transfers between devices, with_halo(): lax.ppermute(tail, axis, [(i, (i + 1) % count) for i in range(ends)])  8.32 us
    slice x12, local copies, waits for them, and re-layouts, plane_conv(): total[..., :span].reshape(total.shape[:-1] + (inner, side))[..., :inner]  7.78 us
  transfers between devices with their start and end apart: 6, of which 6 were waited for; matrix products, arithmetic and copies ran while one was open for 7% of the time, Pallas kernels for 0%

commit v1 on v0

v1 whole, which is shorter than its diff:
```python
import functools

import jax
import jax.numpy as jnp
from jax import lax
from jax.experimental import pallas as pl
from jax.experimental.pallas import tpu as pltpu
from jax.sharding import PartitionSpec as P


F32, BF16 = jnp.float32, jnp.bfloat16
MESH = pl.DeviceIdType.MESH
RIGHT, LEFT = 0, 1
NW, N, NE, W, E, SW, S, SE = range(8)
TOP, BOTTOM, ROWS2, FIRST, LAST, COLS2 = range(6)


def iota(shape, dim):
    return lax.broadcasted_iota(jnp.int32, shape, dim)


def turn(x, k):
    k %= 16
    return pltpu.roll(x, k, 0) if k else x


def dot(a, b, ca=1, cb=0):
    return lax.dot_general(a, b, (((ca,), (cb,)), ((), ())), preferred_element_type=F32)


def row_strip(slab, a):
    row = iota((16, 1), 0)
    out = turn(slab(0), -4 * a)
    for j in range(1, 4):
        out = jnp.where(row // 4 == j, turn(slab(j), 4 * j - 4 * a), out)
    return out


def col_strip(slab, b):
    row = iota((16, 1), 0)
    out = turn(slab(0), -b)
    for i in range(1, 4):
        out = jnp.where(row % 4 == i, turn(slab(i), i - b), out)
    return out


def strip_halves(slab, wide):
    low = iota((16, 128), 1) < 64
    out = {}
    for half in range(2):
        out[TOP, half] = row_strip(lambda j: slab(0, j, half), 0)
        out[BOTTOM, half] = row_strip(lambda j: slab(3, j, half), 3)
        out[FIRST, half] = col_strip(lambda i: slab(i, 0, half), 0)
        out[LAST, half] = col_strip(lambda i: slab(i, 3, half), 3)
        if wide:
            if half == 0:
                out[ROWS2, half] = row_strip(lambda j: slab(1, j, half), 0)
            else:
                out[ROWS2, half] = row_strip(lambda j: slab(2, j, half), 3)
            out[COLS2, half] = jnp.where(
                low, col_strip(lambda i: slab(i, 1, half), 0), col_strip(lambda i: slab(i, 2, half), 3)
            )
    return out


def surround(slab, strip, width, emit):
    row = iota((16, 1), 0)
    first, last = row % 4 == 0, row % 4 == 3
    top, bottom = row < 4, row >= 12
    cols = range(-width, 4 + width)
    for half in range(2):

        def widened(i):
            out = {j: slab(i, j, half) for j in range(4)}
            for j in cols:
                if j == -1:
                    out[j] = jnp.where(first, turn(strip(W, LAST, half), -i), turn(slab(i, 3, half), 1))
                if j == -2:
                    out[j] = jnp.where(first, turn(strip(W, COLS2, half), -i), turn(slab(i, 2, half), 1))
                if j == 4:
                    out[j] = jnp.where(last, turn(strip(E, FIRST, half), 3 - i), turn(slab(i, 0, half), -1))
                if j == 5:
                    out[j] = jnp.where(last, turn(strip(E, COLS2, half), 3 - i), turn(slab(i, 1, half), -1))
            return out

        def beyond(kind, mid, before, after, base, j):
            own = strip(mid, kind, half)
            if 0 <= j < 4:
                return turn(own, base - 4 * j)
            if j == -1:
                return jnp.where(first, turn(strip(before, kind, half), base + 1), turn(own, base - 11))
            if j == -2:
                return jnp.where(first, turn(strip(before, kind, half), base - 11), turn(own, base - 7))
            if j == 4:
                return jnp.where(last, turn(strip(after, kind, half), base + 3), turn(own, base - 1))
            return jnp.where(last, turn(strip(after, kind, half), base - 1), turn(own, base - 5))

        for i in range(4):
            line = widened(i)
            emit(i, half, [line[j] for j in cols])
            if i == 0:
                emit(4, half, [
                    jnp.where(bottom, beyond(TOP, S, SW, SE, 12, j), turn(line[j], -4)) for j in cols
                ])
            if i == 1 and width == 2 and half == 0:
                emit(5, half, [
                    jnp.where(bottom, beyond(ROWS2, S, SW, SE, 12, j), turn(line[j], -4)) for j in cols
                ])
            if i == 2 and width == 2 and half == 1:
                emit(-2, half, [
                    jnp.where(top, beyond(ROWS2, N, NW, NE, 0, j), turn(line[j], 4)) for j in cols
                ])
            if i == 3:
                emit(-1, half, [
                    jnp.where(top, beyond(BOTTOM, N, NW, NE, 0, j), turn(line[j], 4)) for j in cols
                ])


def emit_odd(store, width, side):
    def emit(row, half, slabs):
        low = iota((16, 128), 1) < 64
        i = row + width - (1 - half)
        if 0 <= i < side:
            for j in range(side):
                store(i, j, half, jnp.where(low, slabs[j + 1], slabs[j]))

    return emit


def body(
    n_depth, n_plane,
    act, pw, pb, dw, db, cnt, nbr, vm, out,
    sel, hid, msk, x_in, y1, y2, branch, m1, m2, weights, dweights,
    pool0, pool1, mpool, rim, rim_in, rim_mask, full_in,
    ring_ss, ring_rs, sib_ss, sib_rs, rim_ss, rim_rs, full_ss, full_rs,
):
    n_z = n_plane // 2
    half_z = n_z // 2
    pools = (pool0, pool1)
    d = lax.axis_index("depth")
    p = lax.axis_index("plane")
    z, c = p // 2, p % 2

    def z_at(offset):
        return lax.rem(z + offset + n_z, n_z)

    def plane_id(offset, core):
        return z_at(offset) * 2 + core

    def depth_id(way):
        return lax.rem(d + (1 if way == 0 else n_depth - 1), n_depth)

    barrier = pltpu.get_barrier_semaphore()
    for target in (
        {"plane": plane_id(1, c)}, {"plane": plane_id(-1, c)}, {"plane": z * 2 + 1 - c},
        {"depth": depth_id(0)}, {"depth": depth_id(1)},
    ):
        pl.semaphore_signal(barrier, inc=1, device_id=target, device_id_type=MESH)

    def block_ref(g, owner, item):
        return mpool.at[owner] if item == 2 else pools[g].at[2 * owner + item]

    def ring_copy(g, way, step, item, owner_offset):
        ref = block_ref(g, plane_id(owner_offset, c), item)
        return pltpu.make_async_remote_copy(
            src_ref=ref, dst_ref=ref, send_sem=ring_ss.at[g, way, step, item], recv_sem=ring_rs.at[g, way, step, item],
            device_id={"plane": plane_id(1 if way == RIGHT else -1, c)}, device_id_type=MESH,
        )

    def ring_out(g, way, step, item):
        return ring_copy(g, way, step, item, -step if way == RIGHT else step)

    def ring_in(g, way, step, item):
        return ring_copy(g, way, step, item, -step - 1 if way == RIGHT else step + 1)

    def sib_copy(g, way, step, item, core):
        owner = plane_id(-step - 1 if way == RIGHT else step + 1, core)
        key = 0 if step < 0 else 1 + way * half_z + step
        ref = block_ref(g, owner, item)
        return pltpu.make_async_remote_copy(
            src_ref=ref, dst_ref=ref, send_sem=sib_ss.at[g, key, item], recv_sem=sib_rs.at[g, key, item],
            device_id={"plane": z * 2 + 1 - c}, device_id_type=MESH,
        )

    def items(g, way, step):
        if step < half_z - 1:
            got = (0, 1)
        else:
            got = (0,) if way == RIGHT else (1,)
        if g == 0 and (step < half_z - 1 or way == RIGHT):
            got += (2,)
        return got

    def launch(g, item):
        for way in (RIGHT, LEFT):
            if item in items(g, way, 0):
                ring_out(g, way, 0, item).start()
        sib_copy(g, RIGHT, -1, item, c).start()

    def pass_on(g, step):
        for item in range(3):
            for way in (RIGHT, LEFT):
                if item in items(g, way, step):
                    ring_in(g, way, step, item).wait_recv()
                    if step + 1 < half_z and item in items(g, way, step + 1):
                        ring_out(g, way, step + 1, item).start()
                    sib_copy(g, way, step, item, c).start()

    def all_steps(g):
        got = [(RIGHT, -1, item) for item in ((0, 1, 2) if g == 0 else (0, 1))]
        for step in range(half_z):
            for way in (RIGHT, LEFT):
                got += [(way, step, item) for item in items(g, way, step)]
        return got

    def collect(g):
        for way, step, item in all_steps(g):
            sib_copy(g, way, step, item, 1 - c).wait_recv()

    def settle(g):
        for way, step, item in all_steps(g):
            sib_copy(g, way, step, item, c).wait_send()
            if step >= 0:
                ring_out(g, way, step, item).wait_send()

    def rim_copy(way, t):
        return pltpu.make_async_remote_copy(
            src_ref=rim.at[t], dst_ref=rim_in.at[way, t], send_sem=rim_ss.at[way, t], recv_sem=rim_rs.at[way, t],
            device_id={"depth": depth_id(way)}, device_id_type=MESH,
        )

    def full_copy(blk, way, t):
        return pltpu.make_async_remote_copy(
            src_ref=branch.at[blk, t], dst_ref=full_in.at[blk, way, t],
            send_sem=full_ss.at[blk, way, t], recv_sem=full_rs.at[blk, way, t],
            device_id={"depth": depth_id(way)}, device_id_type=MESH,
        )

    r = iota((512, 1), 0)
    q, i, j, a, b = r // 128, (r // 32) % 4, (r // 8) % 4, (r // 4) % 2, r % 4
    cell = a * 256 + i * 64 + (q // 2) * 32 + b * 8 + j * 2 + q % 2
    sel[...] = jnp.where(cell == iota((512, 512), 1), 1.0, 0.0).astype(BF16)

    low128 = iota((128, 128), 1) < 64
    low16 = iota((16, 128), 1) < 64
    low64 = iota((64, 128), 1) < 64

    def to_patches(src, dst, live):
        for h in range(2):
            v = dot(sel[...], src[:, h * 512 : (h + 1) * 512], 1, 1)
            v = jnp.where(live > slot, v, 0.0)
            for half in range(2):
                even, odd = (v[(2 * half + k) * 128 : (2 * half + k + 1) * 128] for k in range(2))
                lanes = slice(half * 128, half * 128 + 128)
                rows = slice(h * 8, h * 8 + 8)
                dst[0, :, rows, lanes] = jnp.where(low128, even, pltpu.roll(odd, 64, 1)).reshape(16, 8, 128)
                dst[1, :, rows, lanes] = jnp.where(low128, pltpu.roll(even, 64, 1), odd).reshape(16, 8, 128)

    slot = iota((1, 128), 1) // 64
    to_patches(act[...], hid, cnt[p])

    def half_of(half):
        return slice(half * 128, half * 128 + 128)

    def slab_of(ref, t):
        return lambda i, j, half: ref[t, 4 * i + j, :, half_of(half)]

    for t in range(2):
        for (kind, half), value in strip_halves(slab_of(hid, t), True).items():
            pool0[2 * p + t, kind, :, half_of(half)] = value.astype(BF16)

    pl.semaphore_wait(barrier, 5)
    launch(0, 0)
    launch(0, 1)

    spread = jnp.concatenate(
        [jnp.broadcast_to(vm[t].astype(F32), (64, 1024)) for t in range(2)], axis=0
    ).astype(BF16)
    to_patches(spread, msk, 2)
    lane64 = iota((16, 128), 1) % 64
    mask_out = jnp.zeros((16, 128), F32)
    for t in range(2):
        strips = strip_halves(slab_of(msk, t), True)
        for (kind, half), value in strips.items():
            rim_mask[t, kind, :, half_of(half)] = value
            if kind in (TOP, BOTTOM, FIRST, LAST):
                order = (TOP, BOTTOM, FIRST, LAST).index(kind)
                mask_out = jnp.where(lane64 == half * 8 + t * 4 + order, value, mask_out)
    mpool[p] = mask_out.astype(BF16)
    launch(0, 2)

    def twice(w):
        unit = jnp.where(iota((64, 128), 0) == iota((64, 128), 1) % 64, 1.0, 0.0).astype(BF16)
        return dot(w, unit, 0, 0)

    def plane_weights(blk, layer):
        w = twice(pw[blk, layer])
        mirror_in, mirror_out = layer != 1, layer == 1
        for s in range(4):
            for q in range(4):
                u = 2 * (s // 2) + (1 - q // 2 if mirror_in else q // 2)
                v = 2 * (s % 2) + (1 - q % 2 if mirror_in else q % 2)
                rows = slice((s * 4 + q) * 64, (s * 4 + q + 1) * 64)
                for half in range(2):
                    parts = []
                    for col in range(2):
                        dr = u - (1 - half if mirror_out else half)
                        dc = v - (1 - col if mirror_out else col)
                        ok = 0 <= dr < 3 and 0 <= dc < 3
                        tap = dr * 3 + dc
                        parts.append(w[tap * 64 : (tap + 1) * 64] if ok else jnp.zeros((64, 128), F32))
                    weights[blk * 3 + layer, rows, half_of(half)] = jnp.where(low64, *parts).astype(BF16)

    def depth_weights(blk):
        w = twice(dw[blk])
        zero = jnp.zeros((64, 128), F32)
        for tap in range(3):
            part = w[tap * 64 : (tap + 1) * 64]
            if tap == 0:
                part = jnp.where(d > 0, part, 0.0)
            if tap == 2:
                part = jnp.where(d < n_depth - 1, part, 0.0)
            for q in range(4):
                rows = slice(tap * 256 + q * 64, tap * 256 + (q + 1) * 64)
                mine = jnp.where(low64, part, 0.0) if q % 2 == 0 else jnp.where(low64, 0.0, part)
                for half in range(2):
                    dweights[blk, rows, half_of(half)] = (mine if q // 2 == half else zero).astype(BF16)

    def four(v):
        two = jnp.concatenate([v, v], axis=1)
        return jnp.concatenate([two, two], axis=1)

    plane_weights(0, 0)
    pass_on(0, 0)
    plane_weights(0, 1)
    for step in range(1, half_z):
        pass_on(0, step)
        if step == 1:
            plane_weights(0, 2)
            depth_weights(0)
    collect(0)

    group = {NW: BOTTOM, N: BOTTOM, NE: BOTTOM, W: LAST, E: FIRST, SW: TOP, S: TOP, SE: TOP}

    def around_mask(t, carry):
        spot = iota((16, 128), 1) % 64
        found = {}
        for kind in (TOP, BOTTOM, FIRST, LAST):
            order = (TOP, BOTTOM, FIRST, LAST).index(kind)
            ways = [k for k in range(8) if group[k] == kind]
            rows = []
            for k in ways:
                other = nbr[t, k]
                at = jnp.maximum(other, 0)
                keep = (spot % 8) // 4 == jnp.where(other >= 0, at % 2, 2)
                rows.append(jnp.where(keep, mpool[at // 2].astype(F32), 0.0))
            m, n = iota((128, 256), 0), iota((128, 256), 1)
            hit = (m // 64 == (n % 128) // 64) & ((m % 64) // 8 == n // 128) & (m % 4 == order)
            wide = dot(jnp.concatenate(rows, axis=0).astype(BF16), jnp.where(hit, 1.0, 0.0).astype(BF16))
            for at, k in enumerate(ways):
                found[k] = wide[at * 16 : at * 16 + 16]

        def store_odd(i, j, half, value):
            m2[t, i, j, :, half_of(half)] = value

        odd = emit_odd(store_odd, 1, 5)

        def emit(row, half, slabs):
            for j in range(6):
                m1[t, row + 1, j, :, half_of(half)] = slabs[j]
            odd(row, half, slabs)

        surround(slab_of(msk, t), lambda k, kind, half: found[k][:, half_of(half)], 1, emit)
        return carry

    lax.fori_loop(0, 2, around_mask, 0)

    def conv(blk, layer, src, side, mask, store):
        cells = (side - 1) ** 2
        taps = [
            src[si : si + side - 1, sj : sj + side - 1].reshape(cells * 16, 256)
            for si in range(2)
            for sj in range(2)
        ]
        total = dot(jnp.concatenate(taps, axis=1), weights[blk * 3 + layer])
        total = total + four(pb[blk, layer : layer + 1, :])
        gated = total * (0.5 + 0.5 * jnp.tanh(0.5 * total))
        store((gated * mask.reshape(cells * 16, 256)).astype(BF16))

    def plane_layers(blk):
        def tile(t, carry):
            def store_odd(i, j, half, value):
                x_in[i, j, :, half_of(half)] = value.astype(BF16)

            def strip(k, kind, half):
                other = nbr[t, k]
                value = pools[blk][jnp.maximum(other, 0), kind, :, half_of(half)].astype(F32)
                return jnp.where(other >= 0, value, 0.0)

            surround(slab_of(hid, t), strip, 2, emit_odd(store_odd, 2, 7))

            def to_y1(value):
                y1[...] = value.reshape(6, 6, 16, 256)

            def to_y2(value):
                y2[...] = value.reshape(5, 5, 16, 256)

            def to_branch(value):
                branch[blk, t] = value.reshape(16, 16, 256)

            conv(blk, 0, x_in, 7, m1[t], to_y1)
            conv(blk, 1, y1, 6, m2[t], to_y2)
            conv(blk, 2, y2, 5, msk[t], to_branch)
            if blk == 0:
                slab = lambda i, j, half: branch[0, t, 4 * i + j, :, half_of(half)].astype(F32)
                for (kind, half), value in strip_halves(slab, True).items():
                    rim[t, kind, :, half_of(half)] = value.astype(BF16)
                for way in range(2):
                    rim_copy(way, t).start()
            else:
                for way in range(2):
                    full_copy(1, way, t).start()
            return carry

        lax.fori_loop(0, 2, tile, 0)

    def along_depth(blk, below, own, above):
        return dot(jnp.concatenate([below, own, above], axis=1), dweights[blk]) + four(db[blk : blk + 1, :])

    def residual(blk, t):
        for way in range(2):
            full_copy(blk, way, t).wait_recv()
        total = along_depth(
            blk, full_in[blk, 0, t].reshape(256, 256), branch[blk, t].reshape(256, 256),
            full_in[blk, 1, t].reshape(256, 256),
        )
        new = hid[t].reshape(256, 256) + msk[t].reshape(256, 256) * total
        hid[t] = new.astype(BF16).astype(F32).reshape(16, 16, 256)

    plane_layers(0)
    for t in range(2):
        for way in range(2):
            full_copy(0, way, t).start()
    for t in range(2):
        for way in range(2):
            rim_copy(way, t).wait_recv()
        total = along_depth(
            0, rim_in[0, t].reshape(96, 256), rim[t].reshape(96, 256), rim_in[1, t].reshape(96, 256)
        )
        old = pool0[2 * p + t].astype(F32).reshape(96, 256)
        new = old + rim_mask[t].reshape(96, 256) * total
        pool1[2 * p + t] = new.astype(BF16).reshape(6, 16, 256)
        launch(1, t)
    plane_weights(1, 0)
    pass_on(1, 0)
    plane_weights(1, 1)
    for step in range(1, half_z):
        pass_on(1, step)
        if step == 1:
            plane_weights(1, 2)
            depth_weights(1)
        if step == max(half_z - 2, 1):
            for t in range(2):
                residual(0, t)
    collect(1)
    plane_layers(1)
    for t in range(2):
        residual(1, t)

    for h in range(2):
        parts = []
        for half in range(2):
            lanes, rows = half_of(half), slice(h * 8, h * 8 + 8)
            one = hid[0, :, rows, lanes].reshape(128, 128)
            two = hid[1, :, rows, lanes].reshape(128, 128)
            parts.append(jnp.where(low128, one, pltpu.roll(two, 64, 1)))
            parts.append(jnp.where(low128, pltpu.roll(one, 64, 1), two))
        back = dot(jnp.concatenate(parts, axis=0).astype(BF16), sel[...], 0, 0)
        out[:, h * 512 : (h + 1) * 512] = back.astype(BF16)

    settle(0)
    settle(1)
    for t in range(2):
        for way in range(2):
            rim_copy(way, t).wait_send()
            for blk in range(2):
                full_copy(blk, way, t).wait_send()


def shards(mesh, activations, plane_weight, plane_bias, depth_weight, depth_bias, counts, neighbours, voxel_mask):
    n_depth, n_plane = mesh.shape["depth"], mesh.shape["plane"]
    half_z = n_plane // 4
    vmem = pl.BlockSpec(memory_space=pltpu.VMEM)
    smem = pl.BlockSpec(memory_space=pltpu.SMEM)
    dma = pltpu.SemaphoreType.DMA
    out = pl.pallas_call(
        functools.partial(body, n_depth, n_plane),
        out_shape=jax.ShapeDtypeStruct((128, 1024), BF16),
        in_specs=[vmem] * 5 + [smem, smem, vmem],
        out_specs=vmem,
        scratch_shapes=[
            pltpu.VMEM((512, 512), BF16),
            pltpu.VMEM((2, 16, 16, 256), F32),
            pltpu.VMEM((2, 16, 16, 256), F32),
            pltpu.VMEM((7, 7, 16, 256), BF16),
            pltpu.VMEM((6, 6, 16, 256), BF16),
            pltpu.VMEM((5, 5, 16, 256), BF16),
            pltpu.VMEM((2, 2, 16, 16, 256), BF16),
            pltpu.VMEM((2, 6, 6, 16, 256), F32),
            pltpu.VMEM((2, 5, 5, 16, 256), F32),
            pltpu.VMEM((6, 1024, 256), BF16),
            pltpu.VMEM((2, 768, 256), BF16),
            pltpu.VMEM((2 * n_plane, 6, 16, 256), BF16),
            pltpu.VMEM((2 * n_plane, 6, 16, 256), BF16),
            pltpu.VMEM((n_plane, 16, 128), BF16),
            pltpu.VMEM((2, 6, 16, 256), BF16),
            pltpu.VMEM((2, 2, 6, 16, 256), BF16),
            pltpu.VMEM((2, 6, 16, 256), F32),
            pltpu.VMEM((2, 2, 2, 16, 16, 256), BF16),
            dma((2, 2, half_z, 3)),
            dma((2, 2, half_z, 3)),
            dma((2, 1 + 2 * half_z, 3)),
            dma((2, 1 + 2 * half_z, 3)),
            dma((2, 2)),
            dma((2, 2)),
            dma((2, 2, 2)),
            dma((2, 2, 2)),
        ],
        compiler_params=pltpu.CompilerParams(
            collective_id=0, has_side_effects=True, vmem_limit_bytes=56 * 2**20
        ),
    )(
        activations.reshape(128, 1024), plane_weight, plane_bias, depth_weight, depth_bias, counts, neighbours,
        voxel_mask,
    )
    return out.reshape(activations.shape)


def solution(mesh):
    in_specs = (
        P("plane", "depth", None, None),
        P(),
        P(),
        P(),
        P(),
        P(),
        P("plane", None),
        P("plane", "depth", None),
    )
    out_specs = P("plane", "depth", None, None)
    return jax.shard_map(
        functools.partial(shards, mesh), mesh=mesh, in_specs=in_specs, out_specs=out_specs, check_vma=False
    )
```

time: 198 us -> 71 us (0.36)
  the two profiles are of different devices: /device:TPU:31 before, /device:TPU:1 now
where the time goes in v1:
time: 71 us; the launch traced here: 70.8 us
  Pallas kernels  67.8 us (95%)
  local copies, waits for them, and re-layouts  2.95 us (4%)
    pallas_call x1, Pallas kernels, shards(): pl.pallas_call(functools.partial(body, n_depth, n_plane), out_shape=jax.S...  67.8 us
    unnamed x2, local copies, waits for them, and re-layouts  2.95 us

profile of v1, /device:TPU:1, one launch (start us, length us, event | category | flops | bytes accessed | tf_op | source)
XLA Modules:
  0.0 70.8 jit_solution(4696532442960968240)
XLA Ops:
  0.0 1.3 %copy.9.pb = f32[2,3,64]{2,1,0:T(4,128)} copy(f32[2,3,64]{2,0,1:T(2,128)} %param.10) | data formatting | bytes 3072 | tf_op args[2]
  1.3 67.8 %shard_map.82 = bf16[128,1024]{1,0:T(8,128)(2,1)} custom-call(bf16[128,1024]{1,0:T(8,128)(2,1)} %bitcast.5, bf16[2,3,64,576]{3,2,1,0:T(8,128)(2,1)} %pw.1, f32[2,3,64]{2,1,0:T(4,128)} %copy.9.pb, bf16[2,64,192]{2,1,0:T(8,128)(2,1)} %dw.1, f32[2,64]{1,0:T(2,128)} %db.1, s32[16]{0:T(128)} %cnt.1, s32[2,8]{1,0:T(2,128)} %nbr.1, s32[2,1,1024]{2,1,0:T(1,128)} %vm.1), custom_call_target="tpu_custom_call" | custom-call | tf_op jit(solution)/shard_map/pallas_call | solution.py:496
  69.1 1.7 %copy.12 = bf16[2,1,64,1024]{3,2,1,0:T(8,128)(2,1)} copy(bf16[2,1,64,1024]{3,2,1,0:T(8,128)(2,1)} %bitcast.4) | data formatting | bytes 524288

commit v2 on v1

--- a/solution.py
+++ b/solution.py
@@ -11,6 +11,7 @@
 F32, BF16 = jnp.float32, jnp.bfloat16
 MESH = pl.DeviceIdType.MESH
 RIGHT, LEFT = 0, 1
+MASK = 2
 NW, N, NE, W, E, SW, S, SE = range(8)
 TOP, BOTTOM, ROWS2, FIRST, LAST, COLS2 = range(6)
 
@@ -130,12 +131,11 @@
 def body(
     n_depth, n_plane,
     act, pw, pb, dw, db, cnt, nbr, vm, out,
-    sel, hid, msk, x_in, y1, y2, branch, m1, m2, weights, dweights,
+    sel, hid, msk, x_in, y1, y2, y3, branch, m1, m2, weights, dweights,
     pool0, pool1, mpool, rim, rim_in, rim_mask, full_in,
     ring_ss, ring_rs, sib_ss, sib_rs, rim_ss, rim_rs, full_ss, full_rs,
 ):
     n_z = n_plane // 2
-    half_z = n_z // 2
     pools = (pool0, pool1)
     d = lax.axis_index("depth")
     p = lax.axis_index("plane")
@@ -153,79 +153,96 @@
     barrier = pltpu.get_barrier_semaphore()
     for target in (
         {"plane": plane_id(1, c)}, {"plane": plane_id(-1, c)}, {"plane": z * 2 + 1 - c},
+        {"plane": plane_id(2, c)}, {"plane": plane_id(-2, c)},
         {"depth": depth_id(0)}, {"depth": depth_id(1)},
     ):
         pl.semaphore_signal(barrier, inc=1, device_id=target, device_id_type=MESH)
 
     def block_ref(g, owner, item):
-        return mpool.at[owner] if item == 2 else pools[g].at[2 * owner + item]
-
-    def ring_copy(g, way, step, item, owner_offset):
-        ref = block_ref(g, plane_id(owner_offset, c), item)
+        return mpool.at[owner] if item == MASK else pools[g].at[2 * owner + item]
+
+    def ring_copy(g, way, k, m, item, owner_at):
+        sign = -1 if way == RIGHT else 1
+        ref = block_ref(g, plane_id(sign * owner_at, c), item)
         return pltpu.make_async_remote_copy(
-            src_ref=ref, dst_ref=ref, send_sem=ring_ss.at[g, way, step, item], recv_sem=ring_rs.at[g, way, step, item],
-            device_id={"plane": plane_id(1 if way == RIGHT else -1, c)}, device_id_type=MESH,
+            src_ref=ref, dst_ref=ref, send_sem=ring_ss.at[g, way, k + m - 1, item],
+            recv_sem=ring_rs.at[g, way, k + m - 1, item],
+            device_id={"plane": plane_id(-sign * m, c)}, device_id_type=MESH,
         )
 
-    def ring_out(g, way, step, item):
-        return ring_copy(g, way, step, item, -step if way == RIGHT else step)
-
-    def ring_in(g, way, step, item):
-        return ring_copy(g, way, step, item, -step - 1 if way == RIGHT else step + 1)
-
-    def sib_copy(g, way, step, item, core):
-        owner = plane_id(-step - 1 if way == RIGHT else step + 1, core)
-        key = 0 if step < 0 else 1 + way * half_z + step
+    def ring_out(g, way, k, m, item):
+        return ring_copy(g, way, k, m, item, k)
+
+    def ring_in(g, way, dist, item):
+        return ring_copy(g, way, dist - 1, 1, item, dist)
+
+    def sib_copy(g, way, dist, item, core):
+        owner = plane_id(-dist if way == RIGHT else dist, core)
+        key = 0 if dist == 0 else way * 4 + dist
         ref = block_ref(g, owner, item)
         return pltpu.make_async_remote_copy(
             src_ref=ref, dst_ref=ref, send_sem=sib_ss.at[g, key, item], recv_sem=sib_rs.at[g, key, item],
             device_id={"plane": z * 2 + 1 - c}, device_id_type=MESH,
         )
 
-    def items(g, way, step):
-        if step < half_z - 1:
-            got = (0, 1)
-        else:
-            got = (0,) if way == RIGHT else (1,)
-        if g == 0 and (step < half_z - 1 or way == RIGHT):
-            got += (2,)
+    def leads(way):
+        return 0 if way == RIGHT else 1
+
+    def items(g, way, dist):
+        got = (leads(way), 1 - leads(way))
+        if dist == 4:
+            got = got[:1]
+        if g == 0 and (dist < 4 or way == RIGHT):
+            got += (MASK,)
         return got
 
-    def launch(g, item):
-        for way in (RIGHT, LEFT):
-            if item in items(g, way, 0):
-                ring_out(g, way, 0, item).start()
-        sib_copy(g, RIGHT, -1, item, c).start()
-
-    def pass_on(g, step):
-        for item in range(3):
+    def onward(g, way, dist, item):
+        got = []
+        if dist == 2 and item in items(g, way, 4):
+            got.append(ring_out(g, way, 2, 2, item))
+        if dist < 3:
+            got.append(ring_out(g, way, dist, 1, item))
+        return got
+
+    def launch(g, way, item):
+        for copy in onward(g, way, 0, item):
+            copy.start()
+
+    def share(g, item):
+        sib_copy(g, RIGHT, 0, item, c).start()
+
+    def pass_on(g, *dists):
+        order = sorted(
+            (items(g, way, dist).index(item) * 2 if item != MASK else 9, dist, way, item)
+            for dist in dists for way in (RIGHT, LEFT) for item in items(g, way, dist)
+        )
+        for _, dist, way, item in order:
+            ring_in(g, way, dist, item).wait_recv()
+            for copy in onward(g, way, dist, item):
+                copy.start()
+            sib_copy(g, way, dist, item, c).start()
+
+    def everything(g):
+        got = [(RIGHT, 0, item) for item in ((0, 1, MASK) if g == 0 else (0, 1))]
+        return got + [(way, dist, item) for dist in range(1, 5) for way in (RIGHT, LEFT) for item in items(g, way, dist)]
+
+    def collect(g):
+        for way, dist, item in everything(g):
+            sib_copy(g, way, dist, item, 1 - c).wait_recv()
+
+    def settle(g):
+        for way, dist, item in everything(g):
+            sib_copy(g, way, dist, item, c).wait_send()
+        for dist in range(3):
             for way in (RIGHT, LEFT):
-                if item in items(g, way, step):
-                    ring_in(g, way, step, item).wait_recv()
-                    if step + 1 < half_z and item in items(g, way, step + 1):
-                        ring_out(g, way, step + 1, item).start()
-                    sib_copy(g, way, step, item, c).start()
-
-    def all_steps(g):
-        got = [(RIGHT, -1, item) for item in ((0, 1, 2) if g == 0 else (0, 1))]
-        for step in range(half_z):
-            for way in (RIGHT, LEFT):
-                got += [(way, step, item) for item in items(g, way, step)]
-        return got
-
-    def collect(g):
-        for way, step, item in all_steps(g):
-            sib_copy(g, way, step, item, 1 - c).wait_recv()
-
-    def settle(g):
-        for way, step, item in all_steps(g):
-            sib_copy(g, way, step, item, c).wait_send()
-            if step >= 0:
-                ring_out(g, way, step, item).wait_send()
-
-    def rim_copy(way, t):
+                for item in items(g, way, max(dist, 1)):
+                    for copy in onward(g, way, dist, item):
+                        copy.wait_send()
+
+    def rim_copy(blk, way, t):
         return pltpu.make_async_remote_copy(
-            src_ref=rim.at[t], dst_ref=rim_in.at[way, t], send_sem=rim_ss.at[way, t], recv_sem=rim_rs.at[way, t],
+            src_ref=rim.at[blk, t], dst_ref=rim_in.at[blk, way, t],
+            send_sem=rim_ss.at[blk, way, t], recv_sem=rim_rs.at[blk, way, t],
             device_id={"depth": depth_id(way)}, device_id_type=MESH,
         )
 
@@ -269,9 +286,12 @@
         for (kind, half), value in strip_halves(slab_of(hid, t), True).items():
             pool0[2 * p + t, kind, :, half_of(half)] = value.astype(BF16)
 
-    pl.semaphore_wait(barrier, 5)
-    launch(0, 0)
-    launch(0, 1)
+    pl.semaphore_wait(barrier, 7)
+    for part in range(2):
+        launch(0, RIGHT, part)
+        launch(0, LEFT, 1 - part)
+    share(0, 0)
+    share(0, 1)
 
     spread = jnp.concatenate(
         [jnp.broadcast_to(vm[t].astype(F32), (64, 1024)) for t in range(2)], axis=0
@@ -287,7 +307,9 @@
                 order = (TOP, BOTTOM, FIRST, LAST).index(kind)
                 mask_out = jnp.where(lane64 == half * 8 + t * 4 + order, value, mask_out)
     mpool[p] = mask_out.astype(BF16)
-    launch(0, 2)
+    launch(0, RIGHT, MASK)
+    launch(0, LEFT, MASK)
+    share(0, MASK)
 
     def twice(w):
         unit = jnp.where(iota((64, 128), 0) == iota((64, 128), 1) % 64, 1.0, 0.0).astype(BF16)
@@ -330,14 +352,13 @@
         two = jnp.concatenate([v, v], axis=1)
         return jnp.concatenate([two, two], axis=1)
 
-    plane_weights(0, 0)
-    pass_on(0, 0)
-    plane_weights(0, 1)
-    for step in range(1, half_z):
-        pass_on(0, step)
-        if step == 1:
-            plane_weights(0, 2)
-            depth_weights(0)
+    for blk in range(2):
+        for layer in range(3):
+            plane_weights(blk, layer)
+        depth_weights(blk)
+    pass_on(0, 1)
+    pass_on(0, 2)
+    pass_on(0, 3, 4)
     collect(0)
 
     group = {NW: BOTTOM, N: BOTTOM, NE: BOTTOM, W: LAST, E: FIRST, SW: TOP, S: TOP, SE: TOP}
@@ -375,54 +396,59 @@
 
     lax.fori_loop(0, 2, around_mask, 0)
 
-    def conv(blk, layer, src, side, mask, store):
-        cells = (side - 1) ** 2
-        taps = [
-            src[si : si + side - 1, sj : sj + side - 1].reshape(cells * 16, 256)
-            for si in range(2)
-            for sj in range(2)
-        ]
-        total = dot(jnp.concatenate(taps, axis=1), weights[blk * 3 + layer])
-        total = total + four(pb[blk, layer : layer + 1, :])
-        gated = total * (0.5 + 0.5 * jnp.tanh(0.5 * total))
-        store((gated * mask.reshape(cells * 16, 256)).astype(BF16))
-
-    def plane_layers(blk):
-        def tile(t, carry):
-            def store_odd(i, j, half, value):
-                x_in[i, j, :, half_of(half)] = value.astype(BF16)
-
-            def strip(k, kind, half):
-                other = nbr[t, k]
-                value = pools[blk][jnp.maximum(other, 0), kind, :, half_of(half)].astype(F32)
-                return jnp.where(other >= 0, value, 0.0)
-
-            surround(slab_of(hid, t), strip, 2, emit_odd(store_odd, 2, 7))
-
-            def to_y1(value):
-                y1[...] = value.reshape(6, 6, 16, 256)
-
-            def to_y2(value):
-                y2[...] = value.reshape(5, 5, 16, 256)
-
-            def to_branch(value):
-                branch[blk, t] = value.reshape(16, 16, 256)
-
-            conv(blk, 0, x_in, 7, m1[t], to_y1)
-            conv(blk, 1, y1, 6, m2[t], to_y2)
-            conv(blk, 2, y2, 5, msk[t], to_branch)
-            if blk == 0:
-                slab = lambda i, j, half: branch[0, t, 4 * i + j, :, half_of(half)].astype(F32)
-                for (kind, half), value in strip_halves(slab, True).items():
-                    rim[t, kind, :, half_of(half)] = value.astype(BF16)
-                for way in range(2):
-                    rim_copy(way, t).start()
-            else:
-                for way in range(2):
-                    full_copy(1, way, t).start()
-            return carry
-
-        lax.fori_loop(0, 2, tile, 0)
+    def conv(blk, layer, src, side, mask, dst):
+        n = side - 1
+        w = weights.at[blk * 3 + layer]
+        for lo, hi in ((0, (n + 1) // 2), ((n + 1) // 2, n)):
+            rows = (hi - lo) * n * 16
+            total = four(pb[layer, blk : blk + 1, :])
+            for s in range(4):
+                si, sj = s // 2, s % 2
+                tap = src[lo + si : hi + si, sj : sj + n].reshape(rows, 256)
+                total = total + dot(tap, w[256 * s : 256 * s + 256])
+            gated = total * (0.5 + 0.5 * jnp.tanh(0.5 * total)) * mask(lo, hi).reshape(rows, 256)
+            dst[lo:hi] = gated.astype(BF16).reshape(hi - lo, n, 16, 256)
+
+    def plane_layers(blk, tile, halo):
+        def store_odd(i, j, half, value):
+            x_in[i, j, :, half_of(half)] = value.astype(BF16)
+
+        def strip(k, kind, half):
+            if not halo:
+                return jnp.zeros((16, 128), F32)
+            other = nbr[tile, k]
+            value = pools[blk][jnp.maximum(other, 0), kind, :, half_of(half)].astype(F32)
+            return jnp.where(other >= 0, value, 0.0)
+
+        surround(slab_of(hid, tile), strip, 2, emit_odd(store_odd, 2, 7))
+        conv(blk, 0, x_in, 7, lambda lo, hi: m1[tile, lo:hi], y1)
+        conv(blk, 1, y1, 6, lambda lo, hi: m2[tile, lo:hi], y2)
+        conv(blk, 2, y2, 5, lambda lo, hi: msk[tile, 4 * lo : 4 * hi], y3)
+
+    def send_rim(blk, tile):
+        slab = lambda i, j, half: y3[i, j, :, half_of(half)].astype(F32)
+        for (kind, half), value in strip_halves(slab, True).items():
+            rim[blk, tile, kind, :, half_of(half)] = value.astype(BF16)
+        for way in range(2):
+            rim_copy(blk, way, tile).start()
+
+    def first_block(tile, carry):
+        plane_layers(0, tile, True)
+        branch[0, tile] = y3[...]
+        send_rim(0, tile)
+        return carry
+
+    def early_block(tile, carry):
+        plane_layers(1, tile, False)
+        branch[1, tile] = y3[...]
+        for way in range(2):
+            full_copy(1, way, tile).start()
+        return carry
+
+    def second_block(tile, carry):
+        plane_layers(1, tile, True)
+        send_rim(1, tile)
+        return carry
 
     def along_depth(blk, below, own, above):
         return dot(jnp.concatenate([below, own, above], axis=1), dweights[blk]) + four(db[blk : blk + 1, :])
@@ -437,35 +463,62 @@
         new = hid[t].reshape(256, 256) + msk[t].reshape(256, 256) * total
         hid[t] = new.astype(BF16).astype(F32).reshape(16, 16, 256)
 
-    plane_layers(0)
+    def rim_residual(blk, t):
+        for way in range(2):
+            rim_copy(blk, way, t).wait_recv()
+        total = along_depth(
+            blk, rim_in[blk, 0, t].reshape(96, 256), rim[blk, t].reshape(96, 256), rim_in[blk, 1, t].reshape(96, 256)
+        )
+        old = pools[blk][2 * p + t].astype(F32).reshape(96, 256)
+        return (old + rim_mask[t].reshape(96, 256) * total).astype(BF16).reshape(6, 16, 256)
+
+    def put_rim(t, strips):
+        row = iota((16, 1), 0)
+        first, last, top, bottom = row % 4 == 0, row % 4 == 3, row < 4, row >= 12
+        high16 = iota((16, 128), 1) >= 64
+        for half in range(2):
+            kinds = [strips[kind, :, half_of(half)].astype(F32) for kind in range(6)]
+            for i in range(4):
+                for j in range(4):
+                    value = new = hid[t, 4 * i + j, :, half_of(half)]
+                    if j == 0:
+                        new = jnp.where(first, turn(kinds[FIRST], -i), new)
+                    if j == 3:
+                        new = jnp.where(last, turn(kinds[LAST], 3 - i), new)
+                    if j == 1:
+                        new = jnp.where(first, jnp.where(high16, value, turn(kinds[COLS2], -i)), new)
+                    if j == 2:
+                        new = jnp.where(last, jnp.where(high16, turn(kinds[COLS2], 3 - i), value), new)
+                    if i == 0 or (i == 1 and half == 0):
+                        new = jnp.where(top, turn(kinds[TOP if i == 0 else ROWS2], -4 * j), new)
+                    if i == 3 or (i == 2 and half == 1):
+                        new = jnp.where(bottom, turn(kinds[BOTTOM if i == 3 else ROWS2], 12 - 4 * j), new)
+                    if new is not value:
+                        hid[t, 4 * i + j, :, half_of(half)] = new
+
+    lax.fori_loop(0, 2, first_block, 0)
     for t in range(2):
         for way in range(2):
             full_copy(0, way, t).start()
     for t in range(2):
-        for way in range(2):
-            rim_copy(way, t).wait_recv()
-        total = along_depth(
-            0, rim_in[0, t].reshape(96, 256), rim[t].reshape(96, 256), rim_in[1, t].reshape(96, 256)
-        )
-        old = pool0[2 * p + t].astype(F32).reshape(96, 256)
-        new = old + rim_mask[t].reshape(96, 256) * total
-        pool1[2 * p + t] = new.astype(BF16).reshape(6, 16, 256)
-        launch(1, t)
-    plane_weights(1, 0)
-    pass_on(1, 0)
-    plane_weights(1, 1)
-    for step in range(1, half_z):
-        pass_on(1, step)
-        if step == 1:
-            plane_weights(1, 2)
-            depth_weights(1)
-        if step == max(half_z - 2, 1):
-            for t in range(2):
-                residual(0, t)
+        pool1[2 * p + t] = rim_residual(0, t)
+        launch(1, RIGHT if t == 0 else LEFT, t)
+    launch(1, RIGHT, 1)
+    launch(1, LEFT, 0)
+    share(1, 0)
+    share(1, 1)
+    pass_on(1, 1)
+    pass_on(1, 2)
+    for t in range(2):
+        residual(0, t)
+    lax.fori_loop(0, 2, early_block, 0)
+    pass_on(1, 3, 4)
     collect(1)
-    plane_layers(1)
+    lax.fori_loop(0, 2, second_block, 0)
     for t in range(2):
         residual(1, t)
+    for t in range(2):
+        put_rim(t, rim_residual(1, t))
 
     for h in range(2):
         parts = []
@@ -482,14 +535,13 @@
     settle(1)
     for t in range(2):
         for way in range(2):
-            rim_copy(way, t).wait_send()
             for blk in range(2):
+                rim_copy(blk, way, t).wait_send()
                 full_copy(blk, way, t).wait_send()
 
 
 def shards(mesh, activations, plane_weight, plane_bias, depth_weight, depth_bias, counts, neighbours, voxel_mask):
     n_depth, n_plane = mesh.shape["depth"], mesh.shape["plane"]
-    half_z = n_plane // 4
     vmem = pl.BlockSpec(memory_space=pltpu.VMEM)
     smem = pl.BlockSpec(memory_space=pltpu.SMEM)
     dma = pltpu.SemaphoreType.DMA
@@ -505,7 +557,8 @@
             pltpu.VMEM((7, 7, 16, 256), BF16),
             pltpu.VMEM((6, 6, 16, 256), BF16),
             pltpu.VMEM((5, 5, 16, 256), BF16),
-            pltpu.VMEM((2, 2, 16, 16, 256), BF16),
+            pltpu.VMEM((4, 4, 16, 256), BF16),
+            pltpu.VMEM((2, 2, 4, 4, 16, 256), BF16),
             pltpu.VMEM((2, 6, 6, 16, 256), F32),
             pltpu.VMEM((2, 5, 5, 16, 256), F32),
             pltpu.VMEM((6, 1024, 256), BF16),
@@ -513,16 +566,16 @@
             pltpu.VMEM((2 * n_plane, 6, 16, 256), BF16),
             pltpu.VMEM((2 * n_plane, 6, 16, 256), BF16),
             pltpu.VMEM((n_plane, 16, 128), BF16),
-            pltpu.VMEM((2, 6, 16, 256), BF16),
             pltpu.VMEM((2, 2, 6, 16, 256), BF16),
+            pltpu.VMEM((2, 2, 2, 6, 16, 256), BF16),
             pltpu.VMEM((2, 6, 16, 256), F32),
-            pltpu.VMEM((2, 2, 2, 16, 16, 256), BF16),
-            dma((2, 2, half_z, 3)),
-            dma((2, 2, half_z, 3)),
-            dma((2, 1 + 2 * half_z, 3)),
-            dma((2, 1 + 2 * half_z, 3)),
-            dma((2, 2)),
-            dma((2, 2)),
+            pltpu.VMEM((2, 2, 2, 4, 4, 16, 256), BF16),
+            dma((2, 2, 4, 3)),
+            dma((2, 2, 4, 3)),
+            dma((2, 9, 3)),
+            dma((2, 9, 3)),
+            dma((2, 2, 2)),
+            dma((2, 2, 2)),
             dma((2, 2, 2)),
             dma((2, 2, 2)),
         ],
@@ -530,7 +583,7 @@
             collective_id=0, has_side_effects=True, vmem_limit_bytes=56 * 2**20
         ),
     )(
-        activations.reshape(128, 1024), plane_weight, plane_bias, depth_weight, depth_bias, counts, neighbours,
+        activations.reshape(128, 1024), plane_weight, plane_bias.transpose(1, 0, 2), depth_weight, depth_bias, counts, neighbours,
         voxel_mask,
     )
     return out.reshape(activations.shape)

time: 71 us -> 62.8 us (0.88)
  Pallas kernels: 67.8 us -> 61 us
  local copies, waits for them, and re-layouts: 2.95 us -> 1.67 us
    pallas_call x1, Pallas kernels: 67.8 us -> 61 us  [shards(): pl.pallas_call(functools.partial(body, n_depth, n_plane), out_shape=jax.S...]
    unnamed x2 -> x1, local copies, waits for them, and re-layouts: 2.95 us -> 1.67 us
where the time goes in v2:
time: 62.8 us; the launch traced here: 62.6 us
  Pallas kernels  61 us (97%)
  local copies, waits for them, and re-layouts  1.67 us (3%)
    pallas_call x1, Pallas kernels, shards(): pl.pallas_call(functools.partial(body, n_depth, n_plane), out_shape=jax.S...  61 us
    unnamed x1, local copies, waits for them, and re-layouts  1.67 us

profile of v2, /device:TPU:1, one launch (start us, length us, event | category | flops | bytes accessed | tf_op | source)
XLA Modules:
  0.0 62.6 jit_solution(18428211710464978863)
XLA Ops:
  0.0 61.0 %shard_map.82 = bf16[128,1024]{1,0:T(8,128)(2,1)} custom-call(bf16[128,1024]{1,0:T(8,128)(2,1)} %bitcast.6, bf16[2,3,64,576]{3,2,1,0:T(8,128)(2,1)} %pw.1, f32[3,2,64]{2,1,0:T(2,128)} %bitcast.7, bf16[2,64,192]{2,1,0:T(8,128)(2,1)} %dw.1, f32[2,64]{1,0:T(2,128)} %db.1, s32[16]{0:T(128)} %cnt.1, s32[2,8]{1,0:T(2,128)} %nbr.1, s32[2,1,1024]{2,1,0:T(1,128)} %vm.1), custom_call_target="tpu_custom_call" | custom-call | tf_op jit(solution)/shard_map/pallas_call | solution.py:548
  61.0 1.7 %copy.11 = bf16[2,1,64,1024]{3,2,1,0:T(8,128)(2,1)} copy(bf16[2,1,64,1024]{3,2,1,0:T(8,128)(2,1)} %bitcast.5) | data formatting | bytes 524288

commit v3 on v2

--- a/solution.py
+++ b/solution.py
@@ -11,7 +11,7 @@
 F32, BF16 = jnp.float32, jnp.bfloat16
 MESH = pl.DeviceIdType.MESH
 RIGHT, LEFT = 0, 1
-MASK = 2
+MASK = 12
 NW, N, NE, W, E, SW, S, SE = range(8)
 TOP, BOTTOM, ROWS2, FIRST, LAST, COLS2 = range(6)
 
@@ -130,9 +130,10 @@
 
 def body(
     n_depth, n_plane,
-    act, pw, pb, dw, db, cnt, nbr, vm, out,
+    act_any, pw_any, pb, dw_any, db, cnt, nbr, vm_any, out,
+    act, pw, dw, vm, load_sem,
     sel, hid, msk, x_in, y1, y2, y3, branch, m1, m2, weights, dweights,
-    pool0, pool1, mpool, rim, rim_in, rim_mask, full_in,
+    pool0, pool1, rim, rim_in, rim_mask, full_in,
     ring_ss, ring_rs, sib_ss, sib_rs, rim_ss, rim_rs, full_ss, full_rs,
 ):
     n_z = n_plane // 2
@@ -150,24 +151,33 @@
     def depth_id(way):
         return lax.rem(d + (1 if way == 0 else n_depth - 1), n_depth)
 
+    loads = [
+        pltpu.make_async_copy(src, dst, load_sem.at[k])
+        for k, (src, dst) in enumerate(((act_any, act), (vm_any, vm), (pw_any, pw), (dw_any, dw)))
+    ]
+    for load in loads:
+        load.start()
     barrier = pltpu.get_barrier_semaphore()
     for target in (
-        {"plane": plane_id(1, c)}, {"plane": plane_id(-1, c)}, {"plane": z * 2 + 1 - c},
+        {"plane": plane_id(1, 1 - c)}, {"plane": plane_id(-1, 1 - c)}, {"plane": z * 2 + 1 - c},
         {"plane": plane_id(2, c)}, {"plane": plane_id(-2, c)},
         {"depth": depth_id(0)}, {"depth": depth_id(1)},
     ):
         pl.semaphore_signal(barrier, inc=1, device_id=target, device_id_type=MESH)
 
     def block_ref(g, owner, item):
-        return mpool.at[owner] if item == MASK else pools[g].at[2 * owner + item]
+        return pools[g].at[owner, pl.ds(6 * item, 7 if g == 0 and item == 1 else 6)]
+
+    def core_at(dist):
+        return 1 - c if dist % 2 else c
 
     def ring_copy(g, way, k, m, item, owner_at):
         sign = -1 if way == RIGHT else 1
-        ref = block_ref(g, plane_id(sign * owner_at, c), item)
+        ref = block_ref(g, plane_id(sign * owner_at, core_at(owner_at)), item)
         return pltpu.make_async_remote_copy(
             src_ref=ref, dst_ref=ref, send_sem=ring_ss.at[g, way, k + m - 1, item],
             recv_sem=ring_rs.at[g, way, k + m - 1, item],
-            device_id={"plane": plane_id(-sign * m, c)}, device_id_type=MESH,
+            device_id={"plane": plane_id(-sign * m, core_at(m))}, device_id_type=MESH,
         )
 
     def ring_out(g, way, k, m, item):
@@ -176,7 +186,8 @@
     def ring_in(g, way, dist, item):
         return ring_copy(g, way, dist - 1, 1, item, dist)
 
-    def sib_copy(g, way, dist, item, core):
+    def sib_copy(g, way, dist, item, mine):
+        core = core_at(dist) if mine else 1 - core_at(dist)
         owner = plane_id(-dist if way == RIGHT else dist, core)
         key = 0 if dist == 0 else way * 4 + dist
         ref = block_ref(g, owner, item)
@@ -192,8 +203,6 @@
         got = (leads(way), 1 - leads(way))
         if dist == 4:
             got = got[:1]
-        if g == 0 and (dist < 4 or way == RIGHT):
-            got += (MASK,)
         return got
 
     def onward(g, way, dist, item):
@@ -209,30 +218,30 @@
             copy.start()
 
     def share(g, item):
-        sib_copy(g, RIGHT, 0, item, c).start()
+        sib_copy(g, RIGHT, 0, item, True).start()
 
     def pass_on(g, *dists):
         order = sorted(
-            (items(g, way, dist).index(item) * 2 if item != MASK else 9, dist, way, item)
+            (items(g, way, dist).index(item), dist, way, item)
             for dist in dists for way in (RIGHT, LEFT) for item in items(g, way, dist)
         )
         for _, dist, way, item in order:
             ring_in(g, way, dist, item).wait_recv()
             for copy in onward(g, way, dist, item):
                 copy.start()
-            sib_copy(g, way, dist, item, c).start()
+            sib_copy(g, way, dist, item, True).start()
 
     def everything(g):
-        got = [(RIGHT, 0, item) for item in ((0, 1, MASK) if g == 0 else (0, 1))]
+        got = [(RIGHT, 0, item) for item in (0, 1)]
         return got + [(way, dist, item) for dist in range(1, 5) for way in (RIGHT, LEFT) for item in items(g, way, dist)]
 
     def collect(g):
         for way, dist, item in everything(g):
-            sib_copy(g, way, dist, item, 1 - c).wait_recv()
+            sib_copy(g, way, dist, item, False).wait_recv()
 
     def settle(g):
         for way, dist, item in everything(g):
-            sib_copy(g, way, dist, item, c).wait_send()
+            sib_copy(g, way, dist, item, True).wait_send()
         for dist in range(3):
             for way in (RIGHT, LEFT):
                 for item in items(g, way, max(dist, 1)):
@@ -274,6 +283,7 @@
                 dst[1, :, rows, lanes] = jnp.where(low128, pltpu.roll(even, 64, 1), odd).reshape(16, 8, 128)
 
     slot = iota((1, 128), 1) // 64
+    loads[0].wait()
     to_patches(act[...], hid, cnt[p])
 
     def half_of(half):
@@ -284,15 +294,9 @@
 
     for t in range(2):
         for (kind, half), value in strip_halves(slab_of(hid, t), True).items():
-            pool0[2 * p + t, kind, :, half_of(half)] = value.astype(BF16)
-
-    pl.semaphore_wait(barrier, 7)
-    for part in range(2):
-        launch(0, RIGHT, part)
-        launch(0, LEFT, 1 - part)
-    share(0, 0)
-    share(0, 1)
-
+            pool0[p, 6 * t + kind, :, half_of(half)] = value.astype(BF16)
+
+    loads[1].wait()
     spread = jnp.concatenate(
         [jnp.broadcast_to(vm[t].astype(F32), (64, 1024)) for t in range(2)], axis=0
     ).astype(BF16)
@@ -306,10 +310,14 @@
             if kind in (TOP, BOTTOM, FIRST, LAST):
                 order = (TOP, BOTTOM, FIRST, LAST).index(kind)
                 mask_out = jnp.where(lane64 == half * 8 + t * 4 + order, value, mask_out)
-    mpool[p] = mask_out.astype(BF16)
-    launch(0, RIGHT, MASK)
-    launch(0, LEFT, MASK)
-    share(0, MASK)
+    pool0[p, MASK] = jnp.concatenate([mask_out, jnp.zeros((16, 128), F32)], axis=1).astype(BF16)
+
+    pl.semaphore_wait(barrier, 7)
+    for item in range(2):
+        launch(0, RIGHT, item)
+        launch(0, LEFT, 1 - item)
+    share(0, 0)
+    share(0, 1)
 
     def twice(w):
         unit = jnp.where(iota((64, 128), 0) == iota((64, 128), 1) % 64, 1.0, 0.0).astype(BF16)
@@ -352,6 +360,8 @@
         two = jnp.concatenate([v, v], axis=1)
         return jnp.concatenate([two, two], axis=1)
 
+    loads[2].wait()
+    loads[3].wait()
     for blk in range(2):
         for layer in range(3):
             plane_weights(blk, layer)
@@ -374,7 +384,7 @@
                 other = nbr[t, k]
                 at = jnp.maximum(other, 0)
                 keep = (spot % 8) // 4 == jnp.where(other >= 0, at % 2, 2)
-                rows.append(jnp.where(keep, mpool[at // 2].astype(F32), 0.0))
+                rows.append(jnp.where(keep, pool0[at // 2, MASK, :, :128].astype(F32), 0.0))
             m, n = iota((128, 256), 0), iota((128, 256), 1)
             hit = (m // 64 == (n % 128) // 64) & ((m % 64) // 8 == n // 128) & (m % 4 == order)
             wide = dot(jnp.concatenate(rows, axis=0).astype(BF16), jnp.where(hit, 1.0, 0.0).astype(BF16))
@@ -417,7 +427,8 @@
             if not halo:
                 return jnp.zeros((16, 128), F32)
             other = nbr[tile, k]
-            value = pools[blk][jnp.maximum(other, 0), kind, :, half_of(half)].astype(F32)
+            at = jnp.maximum(other, 0)
+            value = pools[blk][at // 2, at % 2 * 6 + kind, :, half_of(half)].astype(F32)
             return jnp.where(other >= 0, value, 0.0)
 
         surround(slab_of(hid, tile), strip, 2, emit_odd(store_odd, 2, 7))
@@ -469,7 +480,7 @@
         total = along_depth(
             blk, rim_in[blk, 0, t].reshape(96, 256), rim[blk, t].reshape(96, 256), rim_in[blk, 1, t].reshape(96, 256)
         )
-        old = pools[blk][2 * p + t].astype(F32).reshape(96, 256)
+        old = pools[blk][p, 6 * t : 6 * t + 6].astype(F32).reshape(96, 256)
         return (old + rim_mask[t].reshape(96, 256) * total).astype(BF16).reshape(6, 16, 256)
 
     def put_rim(t, strips):
@@ -501,7 +512,7 @@
         for way in range(2):
             full_copy(0, way, t).start()
     for t in range(2):
-        pool1[2 * p + t] = rim_residual(0, t)
+        pool1[p, 6 * t : 6 * t + 6] = rim_residual(0, t)
         launch(1, RIGHT if t == 0 else LEFT, t)
     launch(1, RIGHT, 1)
     launch(1, LEFT, 0)
@@ -544,13 +555,19 @@
     n_depth, n_plane = mesh.shape["depth"], mesh.shape["plane"]
     vmem = pl.BlockSpec(memory_space=pltpu.VMEM)
     smem = pl.BlockSpec(memory_space=pltpu.SMEM)
+    hbm = pl.BlockSpec(memory_space=pl.ANY)
     dma = pltpu.SemaphoreType.DMA
     out = pl.pallas_call(
         functools.partial(body, n_depth, n_plane),
         out_shape=jax.ShapeDtypeStruct((128, 1024), BF16),
-        in_specs=[vmem] * 5 + [smem, smem, vmem],
+        in_specs=[hbm, hbm, vmem, hbm, vmem, smem, smem, hbm],
         out_specs=vmem,
         scratch_shapes=[
+            pltpu.VMEM((128, 1024), BF16),
+            pltpu.VMEM(plane_weight.shape, BF16),
+            pltpu.VMEM(depth_weight.shape, BF16),
+            pltpu.VMEM((2, 1, 1024), jnp.int32),
+            dma((4,)),
             pltpu.VMEM((512, 512), BF16),
             pltpu.VMEM((2, 16, 16, 256), F32),
             pltpu.VMEM((2, 16, 16, 256), F32),
@@ -563,17 +580,16 @@
             pltpu.VMEM((2, 5, 5, 16, 256), F32),
             pltpu.VMEM((6, 1024, 256), BF16),
             pltpu.VMEM((2, 768, 256), BF16),
-            pltpu.VMEM((2 * n_plane, 6, 16, 256), BF16),
-            pltpu.VMEM((2 * n_plane, 6, 16, 256), BF16),
-            pltpu.VMEM((n_plane, 16, 128), BF16),
+            pltpu.VMEM((n_plane, 13, 16, 256), BF16),
+            pltpu.VMEM((n_plane, 12, 16, 256), BF16),
             pltpu.VMEM((2, 2, 6, 16, 256), BF16),
             pltpu.VMEM((2, 2, 2, 6, 16, 256), BF16),
             pltpu.VMEM((2, 6, 16, 256), F32),
             pltpu.VMEM((2, 2, 2, 4, 4, 16, 256), BF16),
-            dma((2, 2, 4, 3)),
-            dma((2, 2, 4, 3)),
-            dma((2, 9, 3)),
-            dma((2, 9, 3)),
+            dma((2, 2, 4, 2)),
+            dma((2, 2, 4, 2)),
+            dma((2, 9, 2)),
+            dma((2, 9, 2)),
             dma((2, 2, 2)),
             dma((2, 2, 2)),
             dma((2, 2, 2)),

time: 62.8 us -> 61.9 us (0.986)
  Pallas kernels: 61 us -> 60 us
    pallas_call x1, Pallas kernels: 61 us -> 60 us  [shards(): pl.pallas_call(functools.partial(body, n_depth, n_plane), out_shape=jax.S...]
where the time goes in v3:
time: 61.9 us; the launch traced here: 61.7 us
  Pallas kernels  60 us (97%)
  local copies, waits for them, and re-layouts  1.67 us (3%)
    pallas_call x1, Pallas kernels, shards(): pl.pallas_call(functools.partial(body, n_depth, n_plane), out_shape=jax.S...  60 us
    unnamed x1, local copies, waits for them, and re-layouts  1.67 us

profile of v3, /device:TPU:1, one launch (start us, length us, event | category | flops | bytes accessed | tf_op | source)
XLA Modules:
  0.0 61.7 jit_solution(4844742793684238509)
XLA Ops:
  0.0 60.0 %shard_map.82 = bf16[128,1024]{1,0:T(8,128)(2,1)} custom-call(bf16[128,1024]{1,0:T(8,128)(2,1)} %bitcast.6, bf16[2,3,64,576]{3,2,1,0:T(8,128)(2,1)} %pw_any.1, f32[3,2,64]{2,1,0:T(2,128)} %bitcast.7, bf16[2,64,192]{2,1,0:T(8,128)(2,1)} %dw_any.1, f32[2,64]{1,0:T(2,128)} %db.1, s32[16]{0:T(128)} %cnt.1, s32[2,8]{1,0:T(2,128)} %nbr.1, s32[2,1,1024]{2,1,0:T(1,128)} %vm_any.1), custom_call_target="tpu_custom_call" | custom-call | tf_op jit(solution)/shard_map/pallas_call | solution.py:560
  60.0 1.7 %copy.11 = bf16[2,1,64,1024]{3,2,1,0:T(8,128)(2,1)} copy(bf16[2,1,64,1024]{3,2,1,0:T(8,128)(2,1)} %bitcast.5) | data formatting | bytes 524288

commit v4 on v3

--- a/solution.py
+++ b/solution.py
@@ -132,7 +132,7 @@
     n_depth, n_plane,
     act_any, pw_any, pb, dw_any, db, cnt, nbr, vm_any, out,
     act, pw, dw, vm, load_sem,
-    sel, hid, msk, x_in, y1, y2, y3, branch, m1, m2, weights, dweights,
+    sel, spreads, hid, msk, x_in, y1, y2, y3, branch, m1, m2, weights, dweights,
     pool0, pool1, rim, rim_in, rim_mask, full_in,
     ring_ss, ring_rs, sib_ss, sib_rs, rim_ss, rim_rs, full_ss, full_rs,
 ):
@@ -366,6 +366,10 @@
         for layer in range(3):
             plane_weights(blk, layer)
         depth_weights(blk)
+    m, n = iota((128, 256), 0), iota((128, 256), 1)
+    for order in range(4):
+        hit = (m // 64 == (n % 128) // 64) & ((m % 64) // 8 == n // 128) & (m % 4 == order)
+        spreads[order] = jnp.where(hit, 1.0, 0.0).astype(BF16)
     pass_on(0, 1)
     pass_on(0, 2)
     pass_on(0, 3, 4)
@@ -385,9 +389,7 @@
                 at = jnp.maximum(other, 0)
                 keep = (spot % 8) // 4 == jnp.where(other >= 0, at % 2, 2)
                 rows.append(jnp.where(keep, pool0[at // 2, MASK, :, :128].astype(F32), 0.0))
-            m, n = iota((128, 256), 0), iota((128, 256), 1)
-            hit = (m // 64 == (n % 128) // 64) & ((m % 64) // 8 == n // 128) & (m % 4 == order)
-            wide = dot(jnp.concatenate(rows, axis=0).astype(BF16), jnp.where(hit, 1.0, 0.0).astype(BF16))
+            wide = dot(jnp.concatenate(rows, axis=0).astype(BF16), spreads[order])
             for at, k in enumerate(ways):
                 found[k] = wide[at * 16 : at * 16 + 16]
 
@@ -419,7 +421,7 @@
             gated = total * (0.5 + 0.5 * jnp.tanh(0.5 * total)) * mask(lo, hi).reshape(rows, 256)
             dst[lo:hi] = gated.astype(BF16).reshape(hi - lo, n, 16, 256)
 
-    def plane_layers(blk, tile, halo):
+    def plane_layers(blk, tile, halo, last):
         def store_odd(i, j, half, value):
             x_in[i, j, :, half_of(half)] = value.astype(BF16)
 
@@ -434,31 +436,29 @@
         surround(slab_of(hid, tile), strip, 2, emit_odd(store_odd, 2, 7))
         conv(blk, 0, x_in, 7, lambda lo, hi: m1[tile, lo:hi], y1)
         conv(blk, 1, y1, 6, lambda lo, hi: m2[tile, lo:hi], y2)
-        conv(blk, 2, y2, 5, lambda lo, hi: msk[tile, 4 * lo : 4 * hi], y3)
-
-    def send_rim(blk, tile):
-        slab = lambda i, j, half: y3[i, j, :, half_of(half)].astype(F32)
+        conv(blk, 2, y2, 5, lambda lo, hi: msk[tile, 4 * lo : 4 * hi], last)
+
+    def send_rim(blk, tile, last):
+        slab = lambda i, j, half: last[i, j, :, half_of(half)].astype(F32)
         for (kind, half), value in strip_halves(slab, True).items():
             rim[blk, tile, kind, :, half_of(half)] = value.astype(BF16)
         for way in range(2):
             rim_copy(blk, way, tile).start()
 
     def first_block(tile, carry):
-        plane_layers(0, tile, True)
-        branch[0, tile] = y3[...]
-        send_rim(0, tile)
+        plane_layers(0, tile, True, branch.at[0, tile])
+        send_rim(0, tile, branch.at[0, tile])
         return carry
 
     def early_block(tile, carry):
-        plane_layers(1, tile, False)
-        branch[1, tile] = y3[...]
+        plane_layers(1, tile, False, branch.at[1, tile])
         for way in range(2):
             full_copy(1, way, tile).start()
         return carry
 
     def second_block(tile, carry):
-        plane_layers(1, tile, True)
-        send_rim(1, tile)
+        plane_layers(1, tile, True, y3)
+        send_rim(1, tile, y3)
         return carry
 
     def along_depth(blk, below, own, above):
@@ -569,6 +569,7 @@
             pltpu.VMEM((2, 1, 1024), jnp.int32),
             dma((4,)),
             pltpu.VMEM((512, 512), BF16),
+            pltpu.VMEM((4, 128, 256), BF16),
             pltpu.VMEM((2, 16, 16, 256), F32),
             pltpu.VMEM((2, 16, 16, 256), F32),
             pltpu.VMEM((7, 7, 16, 256), BF16),

time: 61.9 us -> 61.8 us (level)
  no operation moved by 1% of the time
where the time goes in v4:
time: 61.8 us; the launch traced here: 61.6 us
  Pallas kernels  60 us (97%)
  local copies, waits for them, and re-layouts  1.67 us (3%)
    pallas_call x1, Pallas kernels, shards(): pl.pallas_call(functools.partial(body, n_depth, n_plane), out_shape=jax.S...  60 us
    unnamed x1, local copies, waits for them, and re-layouts  1.67 us

profile of v4, /device:TPU:1, one launch (start us, length us, event | category | flops | bytes accessed | tf_op | source)
XLA Modules:
  0.0 61.6 jit_solution(3830284535136162576)
XLA Ops:
  0.0 60.0 %shard_map.82 = bf16[128,1024]{1,0:T(8,128)(2,1)} custom-call(bf16[128,1024]{1,0:T(8,128)(2,1)} %bitcast.6, bf16[2,3,64,576]{3,2,1,0:T(8,128)(2,1)} %pw_any.1, f32[3,2,64]{2,1,0:T(2,128)} %bitcast.7, bf16[2,64,192]{2,1,0:T(8,128)(2,1)} %dw_any.1, f32[2,64]{1,0:T(2,128)} %db.1, s32[16]{0:T(128)} %cnt.1, s32[2,8]{1,0:T(2,128)} %nbr.1, s32[2,1,1024]{2,1,0:T(1,128)} %vm_any.1), custom_call_target="tpu_custom_call" | custom-call | tf_op jit(solution)/shard_map/pallas_call | solution.py:560
  60.0 1.7 %copy.11 = bf16[2,1,64,1024]{3,2,1,0:T(8,128)(2,1)} copy(bf16[2,1,64,1024]{3,2,1,0:T(8,128)(2,1)} %bitcast.5) | data formatting | bytes 524288

commit v5 on v4

--- a/solution.py
+++ b/solution.py
@@ -319,12 +319,12 @@
     share(0, 0)
     share(0, 1)
 
-    def twice(w):
-        unit = jnp.where(iota((64, 128), 0) == iota((64, 128), 1) % 64, 1.0, 0.0).astype(BF16)
+    def twice(w, scale):
+        unit = jnp.where(iota((64, 128), 0) == iota((64, 128), 1) % 64, scale, 0.0).astype(BF16)
         return dot(w, unit, 0, 0)
 
     def plane_weights(blk, layer):
-        w = twice(pw[blk, layer])
+        w = twice(pw[blk, layer], 0.5)
         mirror_in, mirror_out = layer != 1, layer == 1
         for s in range(4):
             for q in range(4):
@@ -342,7 +342,7 @@
                     weights[blk * 3 + layer, rows, half_of(half)] = jnp.where(low64, *parts).astype(BF16)
 
     def depth_weights(blk):
-        w = twice(dw[blk])
+        w = twice(dw[blk], 1.0)
         zero = jnp.zeros((64, 128), F32)
         for tap in range(3):
             part = w[tap * 64 : (tap + 1) * 64]
@@ -413,12 +413,12 @@
         w = weights.at[blk * 3 + layer]
         for lo, hi in ((0, (n + 1) // 2), ((n + 1) // 2, n)):
             rows = (hi - lo) * n * 16
-            total = four(pb[layer, blk : blk + 1, :])
+            half_sum = four(0.5 * pb[layer, blk : blk + 1, :])
             for s in range(4):
                 si, sj = s // 2, s % 2
                 tap = src[lo + si : hi + si, sj : sj + n].reshape(rows, 256)
-                total = total + dot(tap, w[256 * s : 256 * s + 256])
-            gated = total * (0.5 + 0.5 * jnp.tanh(0.5 * total)) * mask(lo, hi).reshape(rows, 256)
+                half_sum = half_sum + dot(tap, w[256 * s : 256 * s + 256])
+            gated = (half_sum + half_sum * jnp.tanh(half_sum)) * mask(lo, hi).reshape(rows, 256)
             dst[lo:hi] = gated.astype(BF16).reshape(hi - lo, n, 16, 256)
 
     def plane_layers(blk, tile, halo, last):

time: 61.8 us -> 61.8 us (level)
  no operation moved by 1% of the time
where the time goes in v5:
time: 61.8 us; the launch traced here: 61.6 us
  Pallas kernels  59.9 us (97%)
  local copies, waits for them, and re-layouts  1.67 us (3%)
    pallas_call x1, Pallas kernels, shards(): pl.pallas_call(functools.partial(body, n_depth, n_plane), out_shape=jax.S...  59.9 us
    unnamed x1, local copies, waits for them, and re-layouts  1.67 us

profile of v5, /device:TPU:1, one launch (start us, length us, event | category | flops | bytes accessed | tf_op | source)
XLA Modules:
  0.0 61.6 jit_solution(7562212310490086803)
XLA Ops:
  0.0 59.9 %shard_map.82 = bf16[128,1024]{1,0:T(8,128)(2,1)} custom-call(bf16[128,1024]{1,0:T(8,128)(2,1)} %bitcast.6, bf16[2,3,64,576]{3,2,1,0:T(8,128)(2,1)} %pw_any.1, f32[3,2,64]{2,1,0:T(2,128)} %bitcast.7, bf16[2,64,192]{2,1,0:T(8,128)(2,1)} %dw_any.1, f32[2,64]{1,0:T(2,128)} %db.1, s32[16]{0:T(128)} %cnt.1, s32[2,8]{1,0:T(2,128)} %nbr.1, s32[2,1,1024]{2,1,0:T(1,128)} %vm_any.1), custom_call_target="tpu_custom_call" | custom-call | tf_op jit(solution)/shard_map/pallas_call | solution.py:560
  59.9 1.7 %copy.11 = bf16[2,1,64,1024]{3,2,1,0:T(8,128)(2,1)} copy(bf16[2,1,64,1024]{3,2,1,0:T(8,128)(2,1)} %bitcast.5) | data formatting | bytes 524288
